TPU v7x, 512 devices: a whole 4x8x8 slice. The times are simulated.
512 devices in a mesh: blk: 256 (over y, x, z), tp: 2 (over core).
Axes of the slice: x: 4, y: 8, z: 8, core: 2. Of those that a mesh axis runs over, the one named last changes fastest.
Arguments:
- document_query: bfloat16 [131072, 2048], P('blk', 'tp'), may hold values from -16 to 16
- document_key: bfloat16 [131072, 512], P('blk', 'tp'), may hold values from -250 to 250
- document_value: bfloat16 [131072, 512], P('blk', 'tp'), may hold values from -6 to 6
- query_token_query: bfloat16 [4, 2048], P(None, 'tp'), may hold values from -6 to 6
- query_token_key: bfloat16 [4, 512], P(None, 'tp'), may hold values from -16 to 16
- query_token_value: bfloat16 [4, 512], P(None, 'tp'), may hold values from -6 to 6
Outputs:
- ctx_out: bfloat16 [131072, 2048], P('blk', 'tp')
- answer: bfloat16 [4, 2048], replicated
All inputs are finite; a program needn't handle non-finite values.
Results may differ from a plain program's by a relative error of at most 0.0046.
Values may be sent and summed in bfloat16 or wider, within the bound.
No kernel may reach another device: no remote copies, remote signals or barrier semaphores. Data moves between devices by JAX's collectives and lax.ppermute only.
A program may use at most 64 MiB of HBM per device.

v0:
```python
import jax
import jax.numpy as jnp
from jax import lax
from jax.sharding import PartitionSpec as P

HEAD_SIZE = 128
QUERY_PER_KEY = 4
QUERY_TOKENS = 4


def from_root(block, axis, owner):
    block = jnp.where(lax.axis_index(axis) == owner, block, jnp.zeros_like(block))
    return lax.psum(block, axis)


def head_attend(q_head, k_head, v_head, allowed):
    scale = float(q_head.shape[-1]) ** (-0.5)
    scores = jnp.einsum("tgd,sd->gts", q_head, k_head, preferred_element_type=jnp.float32) * scale
    scores = jnp.where(allowed[None], scores, -jnp.inf)
    peak = jnp.max(scores, axis=-1, keepdims=True)
    expo = jnp.exp(scores - peak)
    total = jnp.sum(expo, axis=-1)
    probs = expo.astype(jnp.bfloat16)
    mixed = jnp.einsum("gts,sd->gtd", probs, v_head, preferred_element_type=jnp.float32)
    return (peak[..., 0], total, mixed)


def partial_results(query_rows, key_rows, value_rows, allowed):
    peaks, totals, mixes = ([], [], [])
    for group_heads in range(key_rows.shape[1]):
        peak, total, mixed = head_attend(
            query_rows[:, group_heads],
            key_rows[:, group_heads],
            value_rows[:, group_heads],
            allowed,
        )
        peaks.append(peak)
        totals.append(total)
        mixes.append(mixed)
    return (jnp.stack(peaks), jnp.stack(totals), jnp.stack(mixes))


def join_parts(first, second):
    top = jnp.maximum(first[0], second[0])
    left = jnp.exp(first[0] - top)
    right = jnp.exp(second[0] - top)
    return (
        top,
        first[1] * left + second[1] * right,
        first[2] * left[..., None] + second[2] * right[..., None],
    )


def body(
    document_query,
    document_key,
    document_value,
    query_token_query,
    query_token_key,
    query_token_value,
):
    rows = document_key.shape[0]
    heads_kv = document_key.shape[1] // HEAD_SIZE
    anchor_key, anchor_value = (
        from_root(document_key, "blk", 0),
        from_root(document_value, "blk", 0),
    )
    anchor_on = lax.axis_index("blk") > 0
    own_keys = document_key.reshape(rows, heads_kv, HEAD_SIZE)
    own_values = document_value.reshape(rows, heads_kv, HEAD_SIZE)
    all_keys = jnp.concatenate([anchor_key, document_key], 0).reshape(2 * rows, heads_kv, HEAD_SIZE)
    all_values = jnp.concatenate([anchor_value, document_value], 0).reshape(
        2 * rows, heads_kv, HEAD_SIZE
    )
    query_rows = document_query.reshape(rows, heads_kv, QUERY_PER_KEY, HEAD_SIZE)
    line = jnp.arange(rows)[:, None]
    column = jnp.arange(2 * rows)[None, :]
    allowed = jnp.where(column < rows, anchor_on, column - rows <= line)
    outputs = []
    for group_heads in range(heads_kv):
        peak, total, mixed = head_attend(
            query_rows[:, group_heads],
            all_keys[:, group_heads],
            all_values[:, group_heads],
            allowed,
        )
        outputs.append(jnp.transpose(mixed / total[..., None], (1, 0, 2)))
    ctx_out = (
        jnp.stack(outputs, 1)
        .reshape(rows, heads_kv * QUERY_PER_KEY * HEAD_SIZE)
        .astype(jnp.bfloat16)
    )
    fresh_tokens = query_token_query.reshape(QUERY_TOKENS, heads_kv, QUERY_PER_KEY, HEAD_SIZE)
    full = jnp.ones((QUERY_TOKENS, rows), dtype=bool)
    local_peak, local_total, local_mixed = partial_results(fresh_tokens, own_keys, own_values, full)
    peak_all, total_all, mixed_all = (
        lax.all_gather(local_peak[None], "blk", axis=0, tiled=True),
        lax.all_gather(local_total[None], "blk", axis=0, tiled=True),
        lax.all_gather(local_mixed[None], "blk", axis=0, tiled=True),
    )
    top = jnp.max(peak_all, axis=0)
    weight = jnp.exp(peak_all - top)
    total = jnp.sum(total_all * weight, axis=0)
    merged = jnp.sum(mixed_all * weight[..., None], axis=0)
    causal_mask = jnp.arange(QUERY_TOKENS)[:, None] >= jnp.arange(QUERY_TOKENS)[None, :]
    self_part = partial_results(
        fresh_tokens,
        query_token_key.reshape(QUERY_TOKENS, heads_kv, HEAD_SIZE),
        query_token_value.reshape(QUERY_TOKENS, heads_kv, HEAD_SIZE),
        causal_mask,
    )
    top, total, merged = join_parts((top, total, merged), self_part)
    answer_half = (
        jnp.transpose(merged / total[..., None], (2, 0, 1, 3))
        .reshape(QUERY_TOKENS, heads_kv * QUERY_PER_KEY * HEAD_SIZE)
        .astype(jnp.bfloat16)
    )
    answer = lax.all_gather(answer_half, "tp", axis=1, tiled=True)
    return (ctx_out, answer)


def solution(mesh):
    placed = (
        P("blk", "tp"),
        P("blk", "tp"),
        P("blk", "tp"),
        P(None, "tp"),
        P(None, "tp"),
        P(None, "tp"),
    )
    return jax.shard_map(
        body, mesh=mesh, in_specs=placed, out_specs=(P("blk", "tp"), P()), check_vma=False
    )
```

profile of v0, /device:TPU:1, one launch (start us, length us, event | category | flops | bytes accessed | tf_op | source)
XLA Modules:
  0.0 1427.6 jit_solution(891567457132982181)
XLA Ops:
  7.2 0.0 copy-start
  7.2 0.0 all-reduce.3.cloned.1.call-start
  7.2 1.1 copy.48
  8.3 1.1 copy.53
  9.4 0.9 broadcast_select_fusion
  10.3 0.0 all-reduce.3.cloned.1.call-update
  10.3 0.0 all-gather.5.cloned.1.call-start
  10.4 0.7 reshape.195
  11.1 0.2 fusion.62
  11.3 0.2 fusion.61
  11.5 0.2 fusion.37
  11.7 0.1 convolution_bitcast_fusion.3
  11.8 0.2 fusion.39
  12.0 0.1 convolution_bitcast_fusion.2
  12.1 0.6 pad_maximum_fusion.3
  12.8 0.0 all-gather.5.cloned.1.call-update
  12.8 0.1 copy.69
  12.9 0.1 copy.70
  13.0 0.8 fusion.59
  13.9 0.1 copy.72
  14.0 0.1 copy.78
  14.1 0.1 copy.74
  14.2 0.8 fusion.60
  15.0 0.1 copy.71
  15.2 0.1 copy.77
  15.3 0.1 copy.73
  15.4 0.1 copy.75
  15.5 0.1 copy.76
  15.6 2.3 copy.51
  17.9 586.0 %all-gather.1 = f32[512,4,4]{2,1,0:T(4,128)S(1)} all-gather(f32[2,4,4]{2,1,0:T(4,128)S(1)} %pad_maximum_fusion.4), channel_id=3, replica_groups=mesh['blk'=256,'tp'=2] {'blk'}, dimensions={0}, use_global_device_ids=true | all-gather | bytes 32896 | tf_op jit(solution)/shard_map/all_gather | solution.py:97
  603.9 0.3 reduce_max.67
  604.2 570.2 %all-gather.2 = f32[512,4,4]{2,1,0:T(4,128)S(1)} all-gather(f32[2,4,4]{2,1,0:T(4,128)S(1)} %pad_maximum_fusion.6), channel_id=4, replica_groups=mesh['blk'=256,'tp'=2] {'blk'}, dimensions={0}, use_global_device_ids=true | all-gather | bytes 32896 | tf_op jit(solution)/shard_map/all_gather | solution.py:98
  1174.4 0.0 copy-done
  1174.4 0.1 convolution_bitcast_fusion
  1174.5 0.1 convolution_bitcast_fusion.1
  1174.6 0.3 subtract_exponential_fusion.2
  1174.9 0.4 multiply_reduce_fusion.1
  1175.3 1.0 fusion.12
  1176.3 0.0 all-reduce.3.cloned.1.call-done
  1176.4 1.0 pad_maximum_fusion.2
  1177.4 1.0 pad_maximum_fusion.1
  1178.4 2.6 fusion.4
  1181.0 4.4 fusion
  1185.4 1.8 fusion.2
  1187.2 2.5 fusion.32
  1189.8 2.5 fusion.27
  1192.3 0.1 pad_maximum_fusion
  1192.4 1.3 copy.79
  1193.7 0.0 all-gather.5.cloned.1.call-done
  1193.7 4.4 multiply_reduce_fusion
  1198.1 0.1 fusion.45
  1198.2 221.9 %all_gather.15 = bf16[4,2048]{1,0:T(4,128)(2,1)S(1)} all-gather(bf16[4,1024]{1,0:T(4,128)(2,1)S(1)} %bitcast.205), channel_id=1, replica_groups=mesh['blk'=256,'tp'=2] {'tp'}, dimensions={1}, use_global_device_ids=true | all-gather | bytes 24576 | tf_op jit(solution)/shard_map/all_gather | solution.py:118
  1420.2 0.6 copy.99
  (8 shorter events, 0.1 us)
Async XLA Ops:
  7.2 1167.2 %copy-start = (bf16[4,256]{1,0:T(4,128)(2,1)S(1)}, bf16[4,256]{1,0:T(4,128)(2,1)}, u32[]{:S(2)}) copy-start(bf16[4,256]{1,0:T(4,128)(2,1)} %param.11) | copy-start | bytes 6148
  7.2 1169.2 %all-reduce.3.cloned.1.call-start = ((), (), s32[]{:S(2)}) async-start(), calls=%async_computation.1 | async-start | bytes 1048576 | tf_op jit(solution)/shard_map/psum | solution.py:13
  10.3 1183.4 %all-gather.5.cloned.1.call-start = ((), (), s32[]{:S(2)}) async-start(), calls=%async_computation | async-start | bytes 4210688 | tf_op jit(solution)/shard_map/all_gather | solution.py:99
Sparse Core Ops, SparseCore 0:
  13.2 235.3 all-reduce.2
  254.4 123.3 all-gather.4
where the time goes:
time: 1430 us
  blocking collectives  1380 us (97%)
  matrix products  14.7 us (1%)
    all_gather x1, blocking collectives, body(): lax.all_gather(local_peak[None], 'blk', axis=0, tiled=True)  586 us
    all_gather x1, blocking collectives, body(): lax.all_gather(local_total[None], 'blk', axis=0, tiled=True)  570 us
    all_gather x1, blocking collectives, body(): answer = lax.all_gather(answer_half, 'tp', axis=1, tiled=True)  222 us
  transfers between devices with their start and end apart: 2, of which 0 were waited for; matrix products, arithmetic and copies ran while one was open for 2% of the time, Pallas kernels for 0%

commit v1 on v0

v1 whole, which is shorter than its diff:
```python
import math

import jax
import jax.numpy as jnp
from jax import lax
from jax.experimental import pallas as pl
from jax.experimental.pallas import tpu as pltpu
from jax.sharding import Mesh, PartitionSpec as P

HEAD_SIZE = 128
QUERY_PER_KEY = 4
QUERY_TOKENS = 4
SIZES = (8, 4, 8)
NEG = -1e30
F32 = jnp.float32
BF16 = jnp.bfloat16
SCALE = HEAD_SIZE**-0.5
LOG2E = math.log2(math.e)
VMEM_LIMIT = 40 * 1024 * 1024


def dot_nt(a, b):
    return lax.dot_general(a, b, (((1,), (1,)), ((), ())), preferred_element_type=F32)


def block_index():
    return (lax.axis_index("y") * SIZES[1] + lax.axis_index("x")) * SIZES[2] + lax.axis_index("z")


def parts_of(value, count):
    terms = []
    for _ in range(count - 1):
        term = value.astype(BF16).astype(F32)
        terms.append(term)
        value = value - term
    return terms + [value]


def record_rows(peak, total, mixed):
    return parts_of(mixed, 2) + parts_of(peak, 3) + parts_of(total, 2)


def merge_records(ref, count, stride):
    row = lambda k: ref[pl.ds(k, count, stride=stride), :]
    mixed = row(0) + row(1)
    peak = (row(2) + row(3)) + row(4)
    total = row(5) + row(6)
    top = jnp.max(peak, axis=0, keepdims=True)
    weight = jnp.exp(peak - top)
    return (
        top,
        jnp.sum(total * weight, axis=0, keepdims=True),
        jnp.sum(mixed * weight, axis=0, keepdims=True),
    )


def local_kernel(qt_ref, qk_ref, qv_ref, k_ref, v_ref, out_ref, rec_ref, q_ref):
    heads = qt_ref.shape[1] // HEAD_SIZE
    rows = k_ref.shape[0]
    chunk = rows // (heads * QUERY_TOKENS)
    out_ref[:, : k_ref.shape[1]] = k_ref[...]
    out_ref[:, k_ref.shape[1] : 2 * k_ref.shape[1]] = v_ref[...]
    for h in range(heads):
        q_ref[h * QUERY_TOKENS : (h + 1) * QUERY_TOKENS, :] = qt_ref[
            :, h * HEAD_SIZE : (h + 1) * HEAD_SIZE
        ].astype(F32)
    rec_ref[...] = jnp.zeros_like(rec_ref)
    first_block = block_index() == 0
    group = QUERY_PER_KEY * QUERY_TOKENS
    token = lax.broadcasted_iota(jnp.int32, (group, 1), 0) % QUERY_TOKENS
    for kv in range(heads // QUERY_PER_KEY):
        cols = slice(kv * HEAD_SIZE, (kv + 1) * HEAD_SIZE)
        q = q_ref[kv * group : (kv + 1) * group, :]
        scores = dot_nt(q.astype(BF16), k_ref[:, cols]) * SCALE
        peak = jnp.max(scores, axis=-1, keepdims=True)
        new_k = qk_ref[:, cols].astype(F32)
        new_v = qv_ref[:, cols].astype(F32)
        own = []
        for j in range(QUERY_TOKENS):
            s = jnp.sum(q * new_k[j : j + 1, :], axis=-1, keepdims=True) * SCALE
            own.append(jnp.where(jnp.logical_and(token >= j, first_block), s, NEG))
        top = peak
        for s in own:
            top = jnp.maximum(top, s)
        expo = jnp.exp(scores - top)
        total = jnp.sum(expo, axis=-1, keepdims=True)
        mixed = jnp.dot(expo.astype(BF16), v_ref[:, cols], preferred_element_type=F32)
        for j, s in enumerate(own):
            e = jnp.exp(s - top)
            total = total + e
            mixed = mixed + e.astype(BF16).astype(F32) * new_v[j : j + 1, :]
        full = (group, HEAD_SIZE)
        for k, value in enumerate(
            record_rows(jnp.broadcast_to(top, full), jnp.broadcast_to(total, full), mixed)
        ):
            rec_ref[pl.ds(kv * group * chunk + k, group, stride=chunk), :] = value
    out_ref[:, 2 * k_ref.shape[1] :] = rec_ref[...].astype(BF16)


def middle_kernel(peers, copies, last, rec_in_ref, chunk_ref, out_ref, in_ref, rec_ref):
    chunk, width = chunk_ref.shape
    in_ref[...] = rec_in_ref[...].astype(F32)
    peak, total, mixed = merge_records(in_ref, peers, chunk)
    if last:
        rec_ref[...] = jnp.broadcast_to(mixed / total, rec_ref.shape)
    else:
        rec_ref[...] = jnp.zeros_like(rec_ref)
        for k, value in enumerate(record_rows(peak, total, mixed)):
            rec_ref[k : k + 1, :] = value
    record = rec_ref[...].astype(BF16)
    piece = chunk_ref[...]
    for i in range(copies):
        out_ref[i * chunk : (i + 1) * chunk, :width] = piece
        out_ref[i * chunk : (i + 1) * chunk, width:] = record


def middle(received, chunk, width, peers, copies, last):
    def kernel(*refs):
        middle_kernel(peers, copies, last, *refs)

    total = received.shape[1]
    return pl.pallas_call(
        kernel,
        grid=(1,),
        out_shape=jax.ShapeDtypeStruct((copies * chunk, total), BF16),
        in_specs=[
            pl.BlockSpec((peers * chunk, HEAD_SIZE), lambda i: (0, width // HEAD_SIZE)),
            pl.BlockSpec((chunk, width), lambda i: (0, 0)),
        ],
        out_specs=pl.BlockSpec((copies * chunk, total), lambda i: (0, 0)),
        scratch_shapes=[
            pltpu.VMEM((peers * chunk, HEAD_SIZE), F32),
            pltpu.VMEM((chunk, HEAD_SIZE), F32),
        ],
        compiler_params=pltpu.CompilerParams(vmem_limit_bytes=VMEM_LIMIT),
        name="merge_last" if last else "merge_first",
    )(received, received)


def answer_kernel(rec_in_ref, out_ref, in_ref):
    heads = out_ref.shape[1] // HEAD_SIZE
    count = heads * QUERY_TOKENS
    in_ref[...] = rec_in_ref[...].astype(F32)
    rows = in_ref[pl.ds(0, count, stride=in_ref.shape[0] // count), :]
    for h in range(heads):
        out_ref[:, h * HEAD_SIZE : (h + 1) * HEAD_SIZE] = rows[
            h * QUERY_TOKENS : (h + 1) * QUERY_TOKENS
        ].astype(BF16)


def attend_kernel(q_ref, k0_ref, v0_ref, k_ref, v_ref, out_ref):
    rows = q_ref.shape[0]
    step = 128
    off = jnp.where(block_index() > 0, 0.0, -NEG).astype(F32)
    factor = SCALE * LOG2E
    line = lax.broadcasted_iota(jnp.int32, (step, step), 0)
    column = lax.broadcasted_iota(jnp.int32, (step, step), 1)
    k0, v0 = k0_ref[...], v0_ref[...]
    for h in range(q_ref.shape[1] // HEAD_SIZE):
        cols = slice(h * HEAD_SIZE, (h + 1) * HEAD_SIZE)
        for i in range(rows // step):
            at = i * step
            q = q_ref[at : at + step, cols]
            far = dot_nt(q, k0)
            diag = jnp.where(column <= line, dot_nt(q, k_ref[at : at + step, :]), NEG)
            peak = jnp.max(diag, axis=-1, keepdims=True)
            if i:
                near = dot_nt(q, k_ref[:at, :])
                peak = jnp.maximum(peak, jnp.max(near, axis=-1, keepdims=True))
            peak = jnp.maximum(peak, jnp.max(far, axis=-1, keepdims=True) - off)
            base = peak * factor
            e = jnp.exp2(diag * factor - base)
            total = jnp.sum(e, axis=-1, keepdims=True)
            mixed = jnp.dot(
                e.astype(BF16), v_ref[at : at + step, :], preferred_element_type=F32
            )
            if i:
                e = jnp.exp2(near * factor - base)
                total += jnp.sum(e, axis=-1, keepdims=True)
                mixed += jnp.dot(e.astype(BF16), v_ref[:at, :], preferred_element_type=F32)
            e = jnp.exp2(far * factor - (base + off))
            total += jnp.sum(e, axis=-1, keepdims=True)
            mixed += jnp.dot(e.astype(BF16), v0, preferred_element_type=F32)
            out_ref[at : at + step, cols] = (mixed / total).astype(BF16)


def attend(document_query, received, document_key, document_value):
    rows, width = document_query.shape
    heads_kv = document_key.shape[1] // HEAD_SIZE
    per_step = 2
    steps = width // HEAD_SIZE // per_step
    share = steps // heads_kv
    wide = pl.BlockSpec((rows, per_step * HEAD_SIZE), lambda i: (0, i))
    narrow = lambda first: pl.BlockSpec((rows, HEAD_SIZE), lambda i: (0, first + i // share))
    return pl.pallas_call(
        attend_kernel,
        grid=(steps,),
        out_shape=jax.ShapeDtypeStruct((rows, width), BF16),
        in_specs=[wide, narrow(0), narrow(heads_kv), narrow(0), narrow(0)],
        out_specs=wide,
        compiler_params=pltpu.CompilerParams(vmem_limit_bytes=VMEM_LIMIT),
        name="attend",
    )(document_query, received, received, document_key, document_value)


def body(
    document_query,
    document_key,
    document_value,
    query_token_query,
    query_token_key,
    query_token_value,
):
    rows, width = document_key.shape
    plane = SIZES[1] * SIZES[2]
    chunk = rows // plane
    full = 2 * width + HEAD_SIZE
    send = pl.pallas_call(
        local_kernel,
        out_shape=jax.ShapeDtypeStruct((rows, full), BF16),
        scratch_shapes=[
            pltpu.VMEM((rows, HEAD_SIZE), F32),
            pltpu.VMEM((plane, HEAD_SIZE), F32),
        ],
        compiler_params=pltpu.CompilerParams(vmem_limit_bytes=VMEM_LIMIT),
        name="local_parts",
    )(query_token_query, query_token_key, query_token_value, document_key, document_value)
    received = lax.all_to_all(send, ("x", "z"), 0, 0, tiled=True)
    send = middle(received, chunk, 2 * width, plane, SIZES[0], False)
    received = lax.all_to_all(send, "y", 0, 0, tiled=True)
    send = middle(received, chunk, 2 * width, SIZES[0], plane, True)
    received = lax.all_to_all(send, ("x", "z"), 0, 0, tiled=True)
    answer_half = pl.pallas_call(
        answer_kernel,
        grid=(1,),
        out_shape=jax.ShapeDtypeStruct(query_token_query.shape, BF16),
        in_specs=[pl.BlockSpec((rows, HEAD_SIZE), lambda i: (0, 2 * width // HEAD_SIZE))],
        out_specs=pl.BlockSpec(query_token_query.shape, lambda i: (0, 0)),
        scratch_shapes=[pltpu.VMEM((rows, HEAD_SIZE), F32)],
        name="answer_rows",
    )(received)
    answer = lax.all_gather(answer_half, "tp", axis=1, tiled=True)
    ctx_out = attend(document_query, received, document_key, document_value)
    return (ctx_out, answer)


def solution(mesh):
    grid = Mesh(mesh.devices.reshape(SIZES + (-1,)), ("y", "x", "z", "tp"))
    blk = ("y", "x", "z")
    placed = (P(blk, "tp"),) * 3 + (P(None, "tp"),) * 3
    return jax.shard_map(
        body, mesh=grid, in_specs=placed, out_specs=(P(blk, "tp"), P()), check_vma=False
    )
```

time: 1430 us -> 96.9 us (0.07)
  blocking collectives: 1380 us -> 75.7 us
  Pallas kernels: 0 us -> 15.5 us
  matrix products: 14.7 us -> 0 us
    all_gather x2 -> x0, blocking collectives: 1160 us -> none  [the longest x1 586 us: body(): lax.all_gather(local_peak[None], 'blk', axis=0, tiled=True)]
    all_gather x1, blocking collectives: 222 us -> 7.84 us  [body(): answer = lax.all_gather(answer_half, 'tp', axis=1, tiled=True)]
    all_to_all x0 -> x3, blocking collectives: none -> 67.9 us  [the longest x2 53 us: body(): received = lax.all_to_all(send, ('x', 'z'), 0, 0, tiled=True)]
    pallas_call x0 -> x5, Pallas kernels: none -> 15.5 us  [the longest x1 13.1 us: attend(): pl.pallas_call(attend_kernel, grid=(steps,), out_shape=jax.ShapeDtypeStru...]
    dot_general x12 -> x0, matrix products: 14.7 us -> none  [the longest x6 9.1 us: head_attend(): jnp.einsum('tgd,sd->gts', q_head, k_head, preferred_element_type=jnp.floa...]
  transfers between devices with their start and end apart: 2 -> 0, of which waited for: 0 -> 0; matrix products, arithmetic and copies ran while one was open for 2% -> 0% of each run, Pallas kernels for 0% -> 0%
where the time goes in v1:
time: 96.9 us; the launch traced here: 96.6 us
  blocking collectives  75.7 us (78%)
  Pallas kernels  15.5 us (16%)
  local copies, waits for them, and re-layouts  4.58 us (5%)
    all_to_all x2, blocking collectives, body(): received = lax.all_to_all(send, ('x', 'z'), 0, 0, tiled=True)  53 us
    all_to_all x1, blocking collectives, body(): received = lax.all_to_all(send, 'y', 0, 0, tiled=True)  14.9 us
    pallas_call x1, Pallas kernels, attend(): pl.pallas_call(attend_kernel, grid=(steps,), out_shape=jax.ShapeDtypeStru...  13.1 us
    all_gather x1, blocking collectives, body(): answer = lax.all_gather(answer_half, 'tp', axis=1, tiled=True)  7.84 us
    unnamed x21, local copies, waits for them, and re-layouts  4.58 us

profile of v1, /device:TPU:1, one launch (start us, length us, event | category | flops | bytes accessed | tf_op | source)
XLA Modules:
  0.0 96.6 jit_solution(1920269789831009900)
XLA Ops:
  0.6 0.0 copy-start.2
  0.6 0.9 copy-done.2
  1.6 0.0 copy-start.4
  1.6 0.9 copy-done.4
  2.5 0.0 copy-start.6
  2.5 0.7 copy-done.6
  3.2 0.0 copy-start.7
  3.2 0.7 copy-done.7
  3.9 0.0 copy-start.8
  3.9 0.7 copy-done.8
  4.6 0.6 local_parts.1
  5.2 29.9 %all_to_all.33 = bf16[32,16,640]{2,1,0:T(8,128)(2,1)S(1)} all-to-all(bf16[32,16,640]{2,1,0:T(8,128)(2,1)S(1)} %bitcast.12), channel_id=1, replica_groups=mesh['y'=8,'x'=4,'z'=8,'tp'=2] {'x','z'}, dimensions={0} | all-to-all | bytes 1310720 | tf_op jit(solution)/shard_map/all_to_all | solution.py:228
  35.1 0.1 merge_first.1
  35.2 14.9 %all_to_all.34 = bf16[8,16,640]{2,1,0:T(8,128)(2,1)S(1)} all-to-all(bf16[8,16,640]{2,1,0:T(8,128)(2,1)S(1)} %bitcast.15), channel_id=1, replica_groups=mesh['y'=8,'x'=4,'z'=8,'tp'=2] {'y'}, dimensions={0} | all-to-all | bytes 327680 | tf_op jit(solution)/shard_map/all_to_all | solution.py:230
  50.1 0.0 copy-start.5
  50.1 0.1 merge_last.1
  50.2 0.0 copy-start.1
  50.2 0.0 copy-start.3
  50.2 23.1 %all_to_all.35 = bf16[32,16,640]{2,1,0:T(8,128)(2,1)} all-to-all(bf16[32,16,640]{2,1,0:T(8,128)(2,1)S(1)} %bitcast.11), channel_id=1, replica_groups=mesh['y'=8,'x'=4,'z'=8,'tp'=2] {'x','z'}, dimensions={0} | all-to-all | bytes 1310720 | tf_op jit(solution)/shard_map/all_to_all | solution.py:232
  73.4 0.0 copy-start
  73.4 1.6 %answer_rows.1 = bf16[4,1024]{1,0:T(4,128)(2,1)} custom-call(bf16[512,640]{1,0:T(8,128)(2,1)} %bitcast.6), custom_call_target="tpu_custom_call" | custom-call | tf_op jit(solution)/shard_map/answer_rows/pallas_call | solution.py:233
  75.0 0.0 copy-done.5
  75.0 0.0 copy-done.1
  75.0 0.0 copy-done.3
  75.0 0.0 copy-done
  75.0 0.0 copy-start.9
  75.0 13.1 %attend.1 = bf16[512,1024]{1,0:T(8,128)(2,1)} custom-call(bf16[512,1024]{1,0:T(8,128)(2,1)S(1)} %copy-done.1, bf16[512,640]{1,0:T(8,128)(2,1)S(1)} %bitcast.7, bf16[512,640]{1,0:T(8,128)(2,1)S(1)} %bitcast.8, bf16[512,256]{1,0:T(8,128)(2,1)S(1)} %copy-done.3, bf16[512,256]{1,0:T(8,128)(2,1)S(1)} %copy-done.5), custom_call_target="tpu_custom_call" | custom-call | tf_op jit(solution)/shard_map/attend/pallas_call | solution.py:195
  88.1 0.0 copy-done.9
  88.1 7.8 %all_gather.3 = bf16[4,2048]{1,0:T(4,128)(2,1)S(1)} all-gather(bf16[4,1024]{1,0:T(4,128)(2,1)S(1)} %copy-done.9), channel_id=1, replica_groups=mesh['y'=8,'x'=4,'z'=8,'tp'=2] {'tp'}, dimensions={1}, use_global_device_ids=true | all-gather | bytes 24576 | tf_op jit(solution)/shard_map/all_gather | solution.py:242
  96.0 0.6 copy.9
Async XLA Ops:
  0.6 1.0 copy-start.2
  1.6 0.9 copy-start.4
  2.5 0.7 copy-start.6
  3.2 0.7 copy-start.7
  3.9 0.7 copy-start.8
  50.1 24.9 %copy-start.5 = (bf16[512,256]{1,0:T(8,128)(2,1)S(1)}, bf16[512,256]{1,0:T(8,128)(2,1)}, u32[]{:S(2)}) copy-start(bf16[512,256]{1,0:T(8,128)(2,1)} %v_ref.3) | copy-start | bytes 786436
  50.2 24.8 %copy-start.1 = (bf16[512,1024]{1,0:T(8,128)(2,1)S(1)}, bf16[512,1024]{1,0:T(8,128)(2,1)}, u32[]{:S(2)}) copy-start(bf16[512,1024]{1,0:T(8,128)(2,1)} %q_ref.1) | copy-start | bytes 3145732
  50.2 24.7 %copy-start.3 = (bf16[512,256]{1,0:T(8,128)(2,1)S(1)}, bf16[512,256]{1,0:T(8,128)(2,1)}, u32[]{:S(2)}) copy-start(bf16[512,256]{1,0:T(8,128)(2,1)} %k_ref.3) | copy-start | bytes 786436
  73.4 1.6 %copy-start = (bf16[32,16,640]{2,1,0:T(8,128)(2,1)S(1)}, bf16[32,16,640]{2,1,0:T(8,128)(2,1)}, u32[]{:S(2)}) copy-start(bf16[32,16,640]{2,1,0:T(8,128)(2,1)} %all_to_all.35) | copy-start | bytes 1966084
  75.0 13.1 %copy-start.9 = (bf16[4,1024]{1,0:T(4,128)(2,1)S(1)}, bf16[4,1024]{1,0:T(4,128)(2,1)}, u32[]{:S(2)}) copy-start(bf16[4,1024]{1,0:T(4,128)(2,1)} %answer_rows.1) | copy-start | bytes 24580

commit v2 on v1

v2 whole, which is shorter than its diff:
```python
import math

import jax
import jax.numpy as jnp
from jax import lax
from jax.experimental import pallas as pl
from jax.experimental.pallas import tpu as pltpu
from jax.sharding import Mesh, PartitionSpec as P

HEAD_SIZE = 128
QUERY_PER_KEY = 4
QUERY_TOKENS = 4
SIZES = (8, 4, 8)
NEG = -1e30
F32 = jnp.float32
BF16 = jnp.bfloat16
SCALE = HEAD_SIZE**-0.5
LOG2E = math.log2(math.e)
VMEM_LIMIT = 40 * 1024 * 1024


FACTOR = SCALE * LOG2E


def dot_nt(a, b):
    return lax.dot_general(a, b, (((1,), (1,)), ((), ())), preferred_element_type=F32)


def block_index():
    return (lax.axis_index("y") * SIZES[1] + lax.axis_index("x")) * SIZES[2] + lax.axis_index("z")


def parts_of(value, count):
    terms = []
    for _ in range(count - 1):
        term = value.astype(BF16).astype(F32)
        terms.append(term)
        value = value - term
    return terms + [value]


def record_rows(peak, total, mixed):
    return parts_of(mixed, 2) + parts_of(peak, 3) + parts_of(total, 2)


def merge_records(ref, count, stride):
    row = lambda k: ref[pl.ds(k, count, stride=stride), :]
    mixed = row(0) + row(1)
    peak = (row(2) + row(3)) + row(4)
    total = row(5) + row(6)
    top = jnp.max(peak, axis=0, keepdims=True)
    weight = jnp.exp(peak - top)
    return (
        top,
        jnp.sum(total * weight, axis=0, keepdims=True),
        jnp.sum(mixed * weight, axis=0, keepdims=True),
    )


def local_kernel(
    qt_hbm, qk_hbm, qv_hbm, k_hbm, v_hbm, out_ref, qt_ref, qk_ref, qv_ref, rec_ref, q_ref, sems
):
    half, width = k_hbm.shape[0] // 2, k_hbm.shape[1]
    copies = [
        pltpu.make_async_copy(source, target, sems.at[n])
        for n, (source, target) in enumerate(
            [
                (qt_hbm, qt_ref),
                (k_hbm.at[:half, :], out_ref.at[:, :width]),
                (k_hbm.at[half:, :], out_ref.at[:, width : 2 * width]),
                (v_hbm.at[:half, :], out_ref.at[:, 2 * width : 3 * width]),
                (v_hbm.at[half:, :], out_ref.at[:, 3 * width : 4 * width]),
                (qk_hbm, qk_ref),
                (qv_hbm, qv_ref),
            ]
        )
    ]
    for copy in copies:
        copy.start()
    rec_ref[...] = jnp.zeros_like(rec_ref)
    first_block = block_index() == 0
    for copy in copies:
        copy.wait()
    heads = qt_ref.shape[1] // HEAD_SIZE
    chunk = half // (heads * QUERY_TOKENS)
    for h in range(heads):
        q_ref[h * QUERY_TOKENS : (h + 1) * QUERY_TOKENS, :] = qt_ref[
            :, h * HEAD_SIZE : (h + 1) * HEAD_SIZE
        ].astype(F32)
    group = QUERY_PER_KEY * QUERY_TOKENS
    token = lax.broadcasted_iota(jnp.int32, (group, 1), 0) % QUERY_TOKENS
    for kv in range(heads // QUERY_PER_KEY):
        cols = slice(kv * HEAD_SIZE, (kv + 1) * HEAD_SIZE)
        part = lambda n: out_ref[:, n * width + kv * HEAD_SIZE : n * width + (kv + 1) * HEAD_SIZE]
        q = q_ref[kv * group : (kv + 1) * group, :]
        scores = [dot_nt(q.astype(BF16), part(n)) * SCALE for n in range(2)]
        new_k = qk_ref[:, cols].astype(F32)
        new_v = qv_ref[:, cols].astype(F32)
        own = []
        for j in range(QUERY_TOKENS):
            s = jnp.sum(q * new_k[j : j + 1, :], axis=-1, keepdims=True) * SCALE
            own.append(jnp.where(jnp.logical_and(token >= j, first_block), s, NEG))
        top = jnp.max(jnp.maximum(scores[0], scores[1]), axis=-1, keepdims=True)
        for s in own:
            top = jnp.maximum(top, s)
        expo = [jnp.exp(s - top) for s in scores]
        total = jnp.sum(expo[0] + expo[1], axis=-1, keepdims=True)
        mixed = jnp.dot(expo[0].astype(BF16), part(2), preferred_element_type=F32)
        mixed += jnp.dot(expo[1].astype(BF16), part(3), preferred_element_type=F32)
        for j, s in enumerate(own):
            e = jnp.exp(s - top)
            total = total + e
            mixed = mixed + e.astype(BF16).astype(F32) * new_v[j : j + 1, :]
        full = (group, HEAD_SIZE)
        for k, value in enumerate(
            record_rows(jnp.broadcast_to(top, full), jnp.broadcast_to(total, full), mixed)
        ):
            rec_ref[pl.ds(kv * group * chunk + k, group, stride=chunk), :] = value
    out_ref[:, 4 * width :] = rec_ref[...].astype(BF16)


def local_parts(inputs, rows, width):
    half = rows // 2
    full = 4 * width + HEAD_SIZE
    hbm = pl.BlockSpec(memory_space=pltpu.HBM)
    return pl.pallas_call(
        local_kernel,
        out_shape=jax.ShapeDtypeStruct((half, full), BF16),
        in_specs=[hbm] * len(inputs),
        out_specs=pl.BlockSpec(memory_space=pltpu.VMEM),
        scratch_shapes=[pltpu.VMEM(array.shape, BF16) for array in inputs[:3]]
        + [
            pltpu.VMEM((half, HEAD_SIZE), F32),
            pltpu.VMEM((inputs[0].shape[1] // HEAD_SIZE * QUERY_TOKENS, HEAD_SIZE), F32),
            pltpu.SemaphoreType.DMA((7,)),
        ],
        compiler_params=pltpu.CompilerParams(vmem_limit_bytes=VMEM_LIMIT),
        name="local_parts",
    )(*(pltpu.with_memory_space_constraint(array, pltpu.HBM) for array in inputs))


def middle_kernel(last, rec_in_ref, chunk_ref, out_ref, in_ref, rec_ref):
    chunk, width = chunk_ref.shape
    in_ref[...] = rec_in_ref[...].astype(F32)
    peak, total, mixed = merge_records(in_ref, in_ref.shape[0] // chunk, chunk)
    if last:
        rec_ref[...] = jnp.broadcast_to(mixed / total, rec_ref.shape)
    else:
        rec_ref[...] = jnp.zeros_like(rec_ref)
        for k, value in enumerate(record_rows(peak, total, mixed)):
            rec_ref[k : k + 1, :] = value
    record = rec_ref[...].astype(BF16)
    piece = chunk_ref[...]
    for i in range(out_ref.shape[0] // chunk):
        out_ref[i * chunk : (i + 1) * chunk, :width] = piece
        out_ref[i * chunk : (i + 1) * chunk, width:] = record


def middle(received, chunk, copies, last):
    def kernel(*refs):
        middle_kernel(last, *refs)

    rows, total = received.shape
    width = total - HEAD_SIZE
    return pl.pallas_call(
        kernel,
        grid=(1,),
        out_shape=jax.ShapeDtypeStruct((copies * chunk, total), BF16),
        in_specs=[
            pl.BlockSpec((rows, HEAD_SIZE), lambda i: (0, width // HEAD_SIZE)),
            pl.BlockSpec((chunk, width), lambda i: (0, 0)),
        ],
        out_specs=pl.BlockSpec((copies * chunk, total), lambda i: (0, 0)),
        scratch_shapes=[
            pltpu.VMEM((rows, HEAD_SIZE), F32),
            pltpu.VMEM((chunk, HEAD_SIZE), F32),
        ],
        compiler_params=pltpu.CompilerParams(vmem_limit_bytes=VMEM_LIMIT),
        name="merge_last" if last else "merge_first",
    )(received, received)


def answer_kernel(rec_in_ref, out_ref, in_ref):
    heads = out_ref.shape[1] // HEAD_SIZE
    count = heads * QUERY_TOKENS
    in_ref[...] = rec_in_ref[...].astype(F32)
    found = in_ref[pl.ds(0, count, stride=in_ref.shape[0] // count), :]
    for h in range(heads):
        out_ref[:, h * HEAD_SIZE : (h + 1) * HEAD_SIZE] = found[
            h * QUERY_TOKENS : (h + 1) * QUERY_TOKENS
        ].astype(BF16)


def answer_rows(received, width):
    rows, total = received.shape
    shape = (QUERY_TOKENS, width)
    return pl.pallas_call(
        answer_kernel,
        grid=(1,),
        out_shape=jax.ShapeDtypeStruct(shape, BF16),
        in_specs=[pl.BlockSpec((rows, HEAD_SIZE), lambda i: (0, total // HEAD_SIZE - 1))],
        out_specs=pl.BlockSpec(shape, lambda i: (0, 0)),
        scratch_shapes=[pltpu.VMEM((rows, HEAD_SIZE), F32)],
        compiler_params=pltpu.CompilerParams(vmem_limit_bytes=VMEM_LIMIT),
        name="answer_rows",
    )(received)


def lanes(value):
    return jnp.broadcast_to(value, (value.shape[0], HEAD_SIZE))


def top_of(pieces):
    high = pieces[0]
    for piece in pieces[1:]:
        high = jnp.maximum(high, piece)
    return lanes(jnp.max(high, axis=-1, keepdims=True))


def split(scores):
    return [scores[:, c : c + HEAD_SIZE] for c in range(0, scores.shape[1], HEAD_SIZE)]


def exps(pieces, base):
    return jnp.concatenate([jnp.exp2(p * FACTOR - base).astype(BF16) for p in pieces], axis=1)


def with_ones(values):
    return jnp.concatenate([values, jnp.ones_like(values)], axis=1)


STEP = 256


def attend_kernel(step, ahead, q_ref, kv_ref, k_ref, v_ref, out_hbm, out_ref, sems):
    rows = q_ref.shape[0]
    heads = q_ref.shape[1] // HEAD_SIZE
    heads_kv = heads // QUERY_PER_KEY
    off = jnp.where(block_index() > 0, 0.0, -NEG).astype(F32)
    line = lax.broadcasted_iota(jnp.int32, (step, step), 0)
    column = lax.broadcasted_iota(jnp.int32, (step, step), 1)
    keep = column <= line
    head = lambda n: slice(n * HEAD_SIZE, (n + 1) * HEAD_SIZE)
    far_values = [with_ones(kv_ref[:, head(2 * heads_kv + n)]) for n in range(2 * heads_kv)]
    values = [with_ones(v_ref[:, head(n)]) for n in range(heads_kv)]
    items = [(h, at) for h in range(heads) for at in range(0, rows, step)]
    copies = []

    def scores_of(h, at):
        kv = h // QUERY_PER_KEY
        q = q_ref[at : at + step, head(h)]
        return (
            dot_nt(q, kv_ref[:, head(kv)]),
            dot_nt(q, kv_ref[:, head(heads_kv + kv)]),
            dot_nt(q, k_ref[: at + step, head(kv)]),
        )

    coming = [scores_of(*item) for item in items[:ahead]]
    for n, (h, at) in enumerate(items):
        if n + ahead < len(items):
            coming.append(scores_of(*items[n + ahead]))
        far_0, far_1, near = coming.pop(0)
        kv = h // QUERY_PER_KEY
        end = at + step
        far = [split(far_0), split(far_1)]
        own = split(near[:, :at]) if at else []
        own += split(jnp.where(keep, near[:, at:], NEG))
        peak = jnp.maximum(top_of(far[0] + far[1]) - off, top_of(own))
        base = peak * FACTOR
        both = jnp.dot(exps(own, base), values[kv][:end], preferred_element_type=F32)
        for side in range(2):
            both += jnp.dot(
                exps(far[side], base + off),
                far_values[side * heads_kv + kv],
                preferred_element_type=F32,
            )
        out_ref[at:end, head(h)] = (both[:, :HEAD_SIZE] * (1.0 / both[:, HEAD_SIZE:])).astype(BF16)
        if end == rows:
            copy = pltpu.make_async_copy(
                out_ref.at[:, head(h)], out_hbm.at[:, head(h)], sems.at[h]
            )
            copy.start()
            copies.append(copy)
    for copy in copies:
        copy.wait()


def attend(document_query, received, document_key, document_value, step=STEP, ahead=1):
    shape = document_query.shape
    vmem = pl.BlockSpec(memory_space=pltpu.VMEM)

    def kernel(*refs):
        attend_kernel(step, ahead, *refs)

    return pl.pallas_call(
        kernel,
        out_shape=jax.ShapeDtypeStruct(shape, BF16),
        in_specs=[vmem] * 4,
        out_specs=pl.BlockSpec(memory_space=pltpu.HBM),
        scratch_shapes=[
            pltpu.VMEM(shape, BF16),
            pltpu.SemaphoreType.DMA((shape[1] // HEAD_SIZE,)),
        ],
        compiler_params=pltpu.CompilerParams(vmem_limit_bytes=VMEM_LIMIT),
        name="attend",
    )(document_query, received, document_key, document_value)


def body(
    document_query,
    document_key,
    document_value,
    query_token_query,
    query_token_key,
    query_token_value,
):
    rows, width = document_key.shape
    plane = SIZES[1] * SIZES[2]
    chunk = rows // 2 // plane
    inputs = (query_token_query, query_token_key, query_token_value, document_key, document_value)
    send = local_parts(inputs, rows, width)
    received = lax.all_to_all(send, ("x", "z"), 0, 0, tiled=True)
    send = middle(received, chunk, SIZES[0], False)
    received = lax.all_to_all(send, "y", 0, 0, tiled=True)
    send = middle(received, chunk, plane, True)
    received = lax.all_to_all(send, ("x", "z"), 0, 0, tiled=True)
    answer_half = answer_rows(received, query_token_query.shape[1])
    other_half = lax.ppermute(answer_half, "tp", [(0, 1), (1, 0)])
    ctx_out = attend(document_query, received, document_key, document_value)
    first = lax.axis_index("tp") == 0
    halves = (
        jnp.where(first, answer_half, other_half),
        jnp.where(first, other_half, answer_half),
    )
    return (ctx_out, jnp.concatenate(halves, axis=1))


def solution(mesh):
    grid = Mesh(mesh.devices.reshape(SIZES + (-1,)), ("y", "x", "z", "tp"))
    blk = ("y", "x", "z")
    placed = (P(blk, "tp"),) * 3 + (P(None, "tp"),) * 3
    return jax.shard_map(
        body, mesh=grid, in_specs=placed, out_specs=(P(blk, "tp"), P()), check_vma=False
    )
```

time: 96.9 us -> 82 us (0.85)
  blocking collectives: 75.7 us -> 64.4 us
  starting transfers between devices: 0 us -> 8.28 us
  Pallas kernels: 15.5 us -> 7.64 us
  local copies, waits for them, and re-layouts: 4.58 us -> 0.01 us
    ppermute x0 -> x1, starting transfers between devices: none -> 8.28 us  [body(): other_half = lax.ppermute(answer_half, 'tp', [(0, 1), (1, 0)])]
    pallas_call x3, Pallas kernels: 15.3 us -> 7.48 us  [the longest x1 5.65 us: attend(): pl.pallas_call(kernel, out_shape=jax.ShapeDtypeStruct(shape, BF16), in_sp...]
    all_gather x1 -> x0, blocking collectives: 7.84 us -> none  [body(): answer = lax.all_gather(answer_half, 'tp', axis=1, tiled=True)]
    unnamed x21 -> x6, local copies, waits for them, and re-layouts: 4.58 us -> 0.01 us
    all_to_all x2, blocking collectives: 53 us -> 49.7 us  [body(): received = lax.all_to_all(send, ('x', 'z'), 0, 0, tiled=True)]
  transfers between devices with their start and end apart: 0 -> 1, of which waited for: 0 -> 0; matrix products, arithmetic and copies ran while one was open for 0% -> 0% of each run, Pallas kernels for 0% -> 7%
where the time goes in v2:
time: 82 us; the launch traced here: 81.7 us
  blocking collectives  64.4 us (79%)
  starting transfers between devices  8.28 us (10%)
  Pallas kernels  7.64 us (9%)
    all_to_all x2, blocking collectives, body(): received = lax.all_to_all(send, ('x', 'z'), 0, 0, tiled=True)  49.7 us
    all_to_all x1, blocking collectives, body(): received = lax.all_to_all(send, 'y', 0, 0, tiled=True)  14.7 us
    ppermute x1, starting transfers between devices, body(): other_half = lax.ppermute(answer_half, 'tp', [(0, 1), (1, 0)])  8.28 us
    pallas_call x1, Pallas kernels, attend(): pl.pallas_call(kernel, out_shape=jax.ShapeDtypeStruct(shape, BF16), in_sp...  5.65 us
    pallas_call x1, Pallas kernels, local_parts(): pl.pallas_call(local_kernel, out_shape=jax.ShapeDtypeStruct((half, full),...  1.8 us
  transfers between devices with their start and end apart: 1, of which 0 were waited for; matrix products, arithmetic and copies ran while one was open for 0% of the time, Pallas kernels for 7%

profile of v2, /device:TPU:1, one launch (start us, length us, event | category | flops | bytes accessed | tf_op | source)
XLA Modules:
  0.0 81.7 jit_solution(5120406142251931983)
XLA Ops:
  0.6 1.8 %local_parts.1 = bf16[256,1152]{1,0:T(8,128)(2,1)S(1)} custom-call(bf16[4,1024]{1,0:T(4,128)(2,1)} %qt_hbm.1, bf16[4,256]{1,0:T(4,128)(2,1)} %qk_hbm.1, bf16[4,256]{1,0:T(4,128)(2,1)} %qv_hbm.1, bf16[512,256]{1,0:T(8,128)(2,1)} %refs_2_.1, bf16[512,256]{1,0:T(8,128)(2,1)} %refs_3_.1), custom_call_target="tpu_custom_call" | custom-call | tf_op jit(solution)/shard_map/local_parts/pallas_call | solution.py:126
  2.4 28.8 %all_to_all.33 = bf16[32,8,1152]{2,1,0:T(8,128)(2,1)S(1)} all-to-all(bf16[32,8,1152]{2,1,0:T(8,128)(2,1)S(1)} %bitcast.11), channel_id=1, replica_groups=mesh['y'=8,'x'=4,'z'=8,'tp'=2] {'x','z'}, dimensions={0} | all-to-all | bytes 1179648 | tf_op jit(solution)/shard_map/all_to_all | solution.py:322
  31.2 0.1 merge_first.1
  31.3 14.7 %all_to_all.34 = bf16[8,8,1152]{2,1,0:T(8,128)(2,1)S(1)} all-to-all(bf16[8,8,1152]{2,1,0:T(8,128)(2,1)S(1)} %bitcast.14), channel_id=1, replica_groups=mesh['y'=8,'x'=4,'z'=8,'tp'=2] {'y'}, dimensions={0} | all-to-all | bytes 294912 | tf_op jit(solution)/shard_map/all_to_all | solution.py:324
  46.0 0.1 merge_last.1
  46.1 0.0 copy-start
  46.1 20.9 %all_to_all.35 = bf16[32,8,1152]{2,1,0:T(8,128)(2,1)S(1)} all-to-all(bf16[32,8,1152]{2,1,0:T(8,128)(2,1)S(1)} %bitcast.10), channel_id=1, replica_groups=mesh['y'=8,'x'=4,'z'=8,'tp'=2] {'x','z'}, dimensions={0} | all-to-all | bytes 1179648 | tf_op jit(solution)/shard_map/all_to_all | solution.py:326
  67.1 0.0 copy-start.1
  67.1 0.0 copy-start.2
  67.1 8.3 %collective-permute-start = (bf16[4,1024]{1,0:T(4,128)(2,1)S(1)}, bf16[4,1024]{1,0:T(4,128)(2,1)S(1)}, u32[]{:S(2)}, u32[]{:S(2)}) collective-permute-start(bf16[4,1024]{1,0:T(4,128)(2,1)S(1)} %answer_rows.1), channel_id=1, source_target_pairs={{0,1},{1,0},{2,3},{3,2},{4,5},{5,4},{6,7},{7,6},{8,9},{9,8},{10,11... | collective-permute-start | bytes 24584 | tf_op jit(solution)/shard_map/ppermute | solution.py:328
  75.4 0.0 copy-done
  75.4 0.0 copy-done.1
  75.4 0.0 copy-done.2
  75.4 5.6 %attend.1 = bf16[512,1024]{1,0:T(8,128)(2,1)} custom-call(bf16[512,1024]{1,0:T(8,128)(2,1)S(1)} %copy-done, bf16[256,1152]{1,0:T(8,128)(2,1)S(1)} %bitcast.7, bf16[512,256]{1,0:T(8,128)(2,1)S(1)} %copy-done.1, bf16[512,256]{1,0:T(8,128)(2,1)S(1)} %copy-done.2), custom_call_target="tpu_custom_call" | custom-call | tf_op jit(solution)/shard_map/attend/pallas_call | solution.py:295
  81.1 0.0 collective-permute-done
  81.1 0.6 pad_maximum_fusion
  (2 shorter events, 0.0 us)
Async XLA Ops:
  46.1 29.3 %copy-start = (bf16[512,1024]{1,0:T(8,128)(2,1)S(1)}, bf16[512,1024]{1,0:T(8,128)(2,1)}, u32[]{:S(2)}) copy-start(bf16[512,1024]{1,0:T(8,128)(2,1)} %refs_0_.1) | copy-start | bytes 3145732
  67.1 8.3 %copy-start.1 = (bf16[512,256]{1,0:T(8,128)(2,1)S(1)}, bf16[512,256]{1,0:T(8,128)(2,1)}, u32[]{:S(2)}) copy-start(bf16[512,256]{1,0:T(8,128)(2,1)} %refs_2_.1) | copy-start | bytes 786436
  67.1 8.4 %copy-start.2 = (bf16[512,256]{1,0:T(8,128)(2,1)S(1)}, bf16[512,256]{1,0:T(8,128)(2,1)}, u32[]{:S(2)}) copy-start(bf16[512,256]{1,0:T(8,128)(2,1)} %refs_3_.1) | copy-start | bytes 786436
  67.1 14.0 %collective-permute-start = (bf16[4,1024]{1,0:T(4,128)(2,1)S(1)}, bf16[4,1024]{1,0:T(4,128)(2,1)S(1)}, u32[]{:S(2)}, u32[]{:S(2)}) collective-permute-start(bf16[4,1024]{1,0:T(4,128)(2,1)S(1)} %answer_rows.1), channel_id=1, source_target_pairs={{0,1},{1,0},{2,3},{3,2},{4,5},{5,4},{6,7},{7,6},{8,9},{9,8},{10,11... | collective-permute-start | bytes 24584 | tf_op jit(solution)/shard_map/ppermute | solution.py:328

commit v3 on v2

--- a/solution.py
+++ b/solution.py
@@ -2,6 +2,7 @@
 
 import jax
 import jax.numpy as jnp
+import numpy as np
 from jax import lax
 from jax.experimental import pallas as pl
 from jax.experimental.pallas import tpu as pltpu
@@ -20,6 +21,23 @@
 
 
 FACTOR = SCALE * LOG2E
+
+
+AXES = ("y", "x", "z", "tp")
+
+
+def exchange_groups():
+    ids = np.arange(2 * math.prod(SIZES)).reshape(SIZES + (2,))
+    y, x, z = SIZES
+    first = np.moveaxis(ids[..., 0], 0, -1).reshape(x * z, y)
+    second = ids[..., 1].reshape(y * x, z)
+    planes = np.concatenate([first.T, second.T]).tolist()
+    lines = np.concatenate([first, second]).tolist()
+    return planes, lines
+
+
+def exchange(array, groups):
+    return lax.all_to_all(array, AXES, 0, 0, tiled=True, axis_index_groups=groups)
 
 
 def dot_nt(a, b):
@@ -315,15 +333,16 @@
     query_token_value,
 ):
     rows, width = document_key.shape
-    plane = SIZES[1] * SIZES[2]
+    planes, lines = exchange_groups()
+    plane = len(planes[0])
     chunk = rows // 2 // plane
     inputs = (query_token_query, query_token_key, query_token_value, document_key, document_value)
     send = local_parts(inputs, rows, width)
-    received = lax.all_to_all(send, ("x", "z"), 0, 0, tiled=True)
-    send = middle(received, chunk, SIZES[0], False)
-    received = lax.all_to_all(send, "y", 0, 0, tiled=True)
+    received = exchange(send, planes)
+    send = middle(received, chunk, len(lines[0]), False)
+    received = exchange(send, lines)
     send = middle(received, chunk, plane, True)
-    received = lax.all_to_all(send, ("x", "z"), 0, 0, tiled=True)
+    received = exchange(send, planes)
     answer_half = answer_rows(received, query_token_query.shape[1])
     other_half = lax.ppermute(answer_half, "tp", [(0, 1), (1, 0)])
     ctx_out = attend(document_query, received, document_key, document_value)

time: 82 us -> 74.7 us (0.911)
  blocking collectives: 64.4 us -> 59.1 us
  starting transfers between devices: 8.28 us -> 6.28 us
    all_to_all x3, blocking collectives: 64.4 us -> 59.1 us  [exchange(): lax.all_to_all(array, AXES, 0, 0, tiled=True, axis_index_groups=groups)]
    ppermute x1, starting transfers between devices: 8.28 us -> 6.28 us  [body(): other_half = lax.ppermute(answer_half, 'tp', [(0, 1), (1, 0)])]
  transfers between devices with their start and end apart: 1 -> 1, of which waited for: 0 -> 0; matrix products, arithmetic and copies ran while one was open for 0% -> 0% of each run, Pallas kernels for 7% -> 8%
where the time goes in v3:
time: 74.7 us; the launch traced here: 74.4 us
  blocking collectives  59.1 us (79%)
  Pallas kernels  7.65 us (10%)
  starting transfers between devices  6.28 us (8%)
    all_to_all x3, blocking collectives, exchange(): lax.all_to_all(array, AXES, 0, 0, tiled=True, axis_index_groups=groups)  59.1 us
    ppermute x1, starting transfers between devices, body(): other_half = lax.ppermute(answer_half, 'tp', [(0, 1), (1, 0)])  6.28 us
    pallas_call x1, Pallas kernels, attend(): pl.pallas_call(kernel, out_shape=jax.ShapeDtypeStruct(shape, BF16), in_sp...  5.65 us
    pallas_call x1, Pallas kernels, local_parts(): pl.pallas_call(local_kernel, out_shape=jax.ShapeDtypeStruct((half, full),...  1.8 us
  transfers between devices with their start and end apart: 1, of which 0 were waited for; matrix products, arithmetic and copies ran while one was open for 0% of the time, Pallas kernels for 8%

profile of v3, /device:TPU:1, one launch (start us, length us, event | category | flops | bytes accessed | tf_op | source)
XLA Modules:
  0.0 74.4 jit_solution(14859451465515508345)
XLA Ops:
  0.6 1.8 %local_parts.1 = bf16[256,1152]{1,0:T(8,128)(2,1)S(1)} custom-call(bf16[4,1024]{1,0:T(4,128)(2,1)} %qt_hbm.1, bf16[4,256]{1,0:T(4,128)(2,1)} %qk_hbm.1, bf16[4,256]{1,0:T(4,128)(2,1)} %qv_hbm.1, bf16[512,256]{1,0:T(8,128)(2,1)} %refs_2_.1, bf16[512,256]{1,0:T(8,128)(2,1)} %refs_3_.1), custom_call_target="tpu_custom_call" | custom-call | tf_op jit(solution)/shard_map/local_parts/pallas_call | solution.py:144
  2.4 23.6 %all_to_all.33 = bf16[32,8,1152]{2,1,0:T(8,128)(2,1)S(1)} all-to-all(bf16[32,8,1152]{2,1,0:T(8,128)(2,1)S(1)} %bitcast.11), channel_id=1, replica_groups={{0,2,4,6,8,10,12,14,16,18,20,22,24,26,28,30,32,34,36,38,40,42,44,46,48,..., dimensions={0} | all-to-all | bytes 1179648 | tf_op jit(solution)/shard_map/all_to_all | solution.py:40
  26.0 0.1 merge_first.1
  26.1 17.9 %all_to_all.34 = bf16[8,8,1152]{2,1,0:T(8,128)(2,1)S(1)} all-to-all(bf16[8,8,1152]{2,1,0:T(8,128)(2,1)S(1)} %bitcast.14), channel_id=1, replica_groups={{0,64,128,192,256,320,384,448},{2,66,130,194,258,322,386,450},{4,68,132..., dimensions={0} | all-to-all | bytes 294912 | tf_op jit(solution)/shard_map/all_to_all | solution.py:40
  44.0 0.1 merge_last.1
  44.1 0.0 copy-start
  44.1 17.7 %all_to_all.35 = bf16[32,8,1152]{2,1,0:T(8,128)(2,1)S(1)} all-to-all(bf16[32,8,1152]{2,1,0:T(8,128)(2,1)S(1)} %bitcast.10), channel_id=1, replica_groups={{0,2,4,6,8,10,12,14,16,18,20,22,24,26,28,30,32,34,36,38,40,42,44,46,48,..., dimensions={0} | all-to-all | bytes 1179648 | tf_op jit(solution)/shard_map/all_to_all | solution.py:40
  61.8 0.0 copy-start.1
  61.8 0.0 copy-start.2
  61.8 6.3 %collective-permute-start = (bf16[4,1024]{1,0:T(4,128)(2,1)S(1)}, bf16[4,1024]{1,0:T(4,128)(2,1)S(1)}, u32[]{:S(2)}, u32[]{:S(2)}) collective-permute-start(bf16[4,1024]{1,0:T(4,128)(2,1)S(1)} %answer_rows.1), channel_id=1, source_target_pairs={{0,1},{1,0},{2,3},{3,2},{4,5},{5,4},{6,7},{7,6},{8,9},{9,8},{10,11... | collective-permute-start | bytes 24584 | tf_op jit(solution)/shard_map/ppermute | solution.py:347
  68.1 0.0 copy-done
  68.1 0.0 copy-done.1
  68.1 0.0 copy-done.2
  68.1 5.7 %attend.1 = bf16[512,1024]{1,0:T(8,128)(2,1)} custom-call(bf16[512,1024]{1,0:T(8,128)(2,1)S(1)} %copy-done, bf16[256,1152]{1,0:T(8,128)(2,1)S(1)} %bitcast.7, bf16[512,256]{1,0:T(8,128)(2,1)S(1)} %copy-done.1, bf16[512,256]{1,0:T(8,128)(2,1)S(1)} %copy-done.2), custom_call_target="tpu_custom_call" | custom-call | tf_op jit(solution)/shard_map/attend/pallas_call | solution.py:313
  73.8 0.0 collective-permute-done
  73.8 0.6 pad_maximum_fusion
  (2 shorter events, 0.0 us)
Async XLA Ops:
  44.1 24.0 %copy-start = (bf16[512,1024]{1,0:T(8,128)(2,1)S(1)}, bf16[512,1024]{1,0:T(8,128)(2,1)}, u32[]{:S(2)}) copy-start(bf16[512,1024]{1,0:T(8,128)(2,1)} %refs_0_.1) | copy-start | bytes 3145732
  61.8 6.3 %copy-start.1 = (bf16[512,256]{1,0:T(8,128)(2,1)S(1)}, bf16[512,256]{1,0:T(8,128)(2,1)}, u32[]{:S(2)}) copy-start(bf16[512,256]{1,0:T(8,128)(2,1)} %refs_2_.1) | copy-start | bytes 786436
  61.8 6.4 %copy-start.2 = (bf16[512,256]{1,0:T(8,128)(2,1)S(1)}, bf16[512,256]{1,0:T(8,128)(2,1)}, u32[]{:S(2)}) copy-start(bf16[512,256]{1,0:T(8,128)(2,1)} %refs_3_.1) | copy-start | bytes 786436
  61.8 12.0 %collective-permute-start = (bf16[4,1024]{1,0:T(4,128)(2,1)S(1)}, bf16[4,1024]{1,0:T(4,128)(2,1)S(1)}, u32[]{:S(2)}, u32[]{:S(2)}) collective-permute-start(bf16[4,1024]{1,0:T(4,128)(2,1)S(1)} %answer_rows.1), channel_id=1, source_target_pairs={{0,1},{1,0},{2,3},{3,2},{4,5},{5,4},{6,7},{7,6},{8,9},{9,8},{10,11... | collective-permute-start | bytes 24584 | tf_op jit(solution)/shard_map/ppermute | solution.py:347

commit v4 on v3

--- a/solution.py
+++ b/solution.py
@@ -76,24 +76,44 @@
 
 
 def local_kernel(
-    qt_hbm, qk_hbm, qv_hbm, k_hbm, v_hbm, out_ref, qt_ref, qk_ref, qv_ref, rec_ref, q_ref, sems
+    qt_hbm,
+    qk_hbm,
+    qv_hbm,
+    k_hbm,
+    v_hbm,
+    out_ref,
+    qt_ref,
+    qk_ref,
+    qv_ref,
+    k_ref,
+    v_ref,
+    rec_ref,
+    q_ref,
+    sems,
 ):
-    half, width = k_hbm.shape[0] // 2, k_hbm.shape[1]
+    rows, width = k_hbm.shape
+    half = rows // 2
+    passed = [
+        pltpu.make_async_copy(
+            k_hbm.at[n * half : (n + 1) * half, :],
+            out_ref.at[:, n * width : (n + 1) * width],
+            sems.at[n],
+        )
+        for n in range(2)
+    ]
     copies = [
-        pltpu.make_async_copy(source, target, sems.at[n])
+        pltpu.make_async_copy(source, target, sems.at[2 + n])
         for n, (source, target) in enumerate(
             [
                 (qt_hbm, qt_ref),
-                (k_hbm.at[:half, :], out_ref.at[:, :width]),
-                (k_hbm.at[half:, :], out_ref.at[:, width : 2 * width]),
-                (v_hbm.at[:half, :], out_ref.at[:, 2 * width : 3 * width]),
-                (v_hbm.at[half:, :], out_ref.at[:, 3 * width : 4 * width]),
+                (k_hbm, k_ref),
+                (v_hbm, v_ref),
                 (qk_hbm, qk_ref),
                 (qv_hbm, qv_ref),
             ]
         )
     ]
-    for copy in copies:
+    for copy in copies + passed:
         copy.start()
     rec_ref[...] = jnp.zeros_like(rec_ref)
     first_block = block_index() == 0
@@ -109,22 +129,20 @@
     token = lax.broadcasted_iota(jnp.int32, (group, 1), 0) % QUERY_TOKENS
     for kv in range(heads // QUERY_PER_KEY):
         cols = slice(kv * HEAD_SIZE, (kv + 1) * HEAD_SIZE)
-        part = lambda n: out_ref[:, n * width + kv * HEAD_SIZE : n * width + (kv + 1) * HEAD_SIZE]
         q = q_ref[kv * group : (kv + 1) * group, :]
-        scores = [dot_nt(q.astype(BF16), part(n)) * SCALE for n in range(2)]
+        scores = dot_nt(q.astype(BF16), k_ref[:, cols]) * SCALE
         new_k = qk_ref[:, cols].astype(F32)
         new_v = qv_ref[:, cols].astype(F32)
         own = []
         for j in range(QUERY_TOKENS):
             s = jnp.sum(q * new_k[j : j + 1, :], axis=-1, keepdims=True) * SCALE
             own.append(jnp.where(jnp.logical_and(token >= j, first_block), s, NEG))
-        top = jnp.max(jnp.maximum(scores[0], scores[1]), axis=-1, keepdims=True)
+        top = jnp.max(scores, axis=-1, keepdims=True)
         for s in own:
             top = jnp.maximum(top, s)
-        expo = [jnp.exp(s - top) for s in scores]
-        total = jnp.sum(expo[0] + expo[1], axis=-1, keepdims=True)
-        mixed = jnp.dot(expo[0].astype(BF16), part(2), preferred_element_type=F32)
-        mixed += jnp.dot(expo[1].astype(BF16), part(3), preferred_element_type=F32)
+        expo = jnp.exp(scores - top)
+        total = jnp.sum(expo, axis=-1, keepdims=True)
+        mixed = jnp.dot(expo.astype(BF16), v_ref[:, cols], preferred_element_type=F32)
         for j, s in enumerate(own):
             e = jnp.exp(s - top)
             total = total + e
@@ -134,19 +152,21 @@
             record_rows(jnp.broadcast_to(top, full), jnp.broadcast_to(total, full), mixed)
         ):
             rec_ref[pl.ds(kv * group * chunk + k, group, stride=chunk), :] = value
-    out_ref[:, 4 * width :] = rec_ref[...].astype(BF16)
-
-
-def local_parts(inputs, rows, width):
+    out_ref[:, 2 * width :] = rec_ref[...].astype(BF16)
+    for copy in passed:
+        copy.wait()
+
+
+def local_parts(inputs):
+    rows, width = inputs[3].shape
     half = rows // 2
-    full = 4 * width + HEAD_SIZE
     hbm = pl.BlockSpec(memory_space=pltpu.HBM)
     return pl.pallas_call(
         local_kernel,
-        out_shape=jax.ShapeDtypeStruct((half, full), BF16),
+        out_shape=jax.ShapeDtypeStruct((half, 2 * width + HEAD_SIZE), BF16),
         in_specs=[hbm] * len(inputs),
         out_specs=pl.BlockSpec(memory_space=pltpu.VMEM),
-        scratch_shapes=[pltpu.VMEM(array.shape, BF16) for array in inputs[:3]]
+        scratch_shapes=[pltpu.VMEM(array.shape, BF16) for array in inputs]
         + [
             pltpu.VMEM((half, HEAD_SIZE), F32),
             pltpu.VMEM((inputs[0].shape[1] // HEAD_SIZE * QUERY_TOKENS, HEAD_SIZE), F32),
@@ -157,8 +177,32 @@
     )(*(pltpu.with_memory_space_constraint(array, pltpu.HBM) for array in inputs))
 
 
-def middle_kernel(last, rec_in_ref, chunk_ref, out_ref, in_ref, rec_ref):
-    chunk, width = chunk_ref.shape
+def passing_on(send, moved, helpers):
+    rows, width = moved.shape
+    half = rows // 2
+
+    def kernel(send_ref, moved_ref, out_ref):
+        position = block_index() * 2 + lax.axis_index("tp")
+
+        @pl.when(jnp.logical_or(position == helpers[0], position == helpers[1]))
+        def _():
+            for n in range(2):
+                out_ref[:, n * width : (n + 1) * width] = moved_ref[n * half : (n + 1) * half, :]
+
+    vmem = pl.BlockSpec(memory_space=pltpu.VMEM)
+    return pl.pallas_call(
+        kernel,
+        out_shape=jax.ShapeDtypeStruct(send.shape, BF16),
+        in_specs=[vmem] * 2,
+        out_specs=vmem,
+        input_output_aliases={0: 0},
+        compiler_params=pltpu.CompilerParams(vmem_limit_bytes=VMEM_LIMIT),
+        name="passing_on",
+    )(send, moved)
+
+
+def middle_kernel(chunk, rec_in_ref, piece_ref, out_ref, in_ref, rec_ref):
+    last = piece_ref.shape[0] == chunk
     in_ref[...] = rec_in_ref[...].astype(F32)
     peak, total, mixed = merge_records(in_ref, in_ref.shape[0] // chunk, chunk)
     if last:
@@ -168,27 +212,32 @@
         for k, value in enumerate(record_rows(peak, total, mixed)):
             rec_ref[k : k + 1, :] = value
     record = rec_ref[...].astype(BF16)
-    piece = chunk_ref[...]
-    for i in range(out_ref.shape[0] // chunk):
-        out_ref[i * chunk : (i + 1) * chunk, :width] = piece
-        out_ref[i * chunk : (i + 1) * chunk, width:] = record
+    width = piece_ref.shape[1]
+    for n in range(piece_ref.shape[0] // chunk):
+        piece = piece_ref[n * chunk : (n + 1) * chunk, :]
+        for at in range(0, out_ref.shape[0], chunk):
+            out_ref[at : at + chunk, n * width : (n + 1) * width] = piece
+    for at in range(0, out_ref.shape[0], chunk):
+        out_ref[at : at + chunk, out_ref.shape[1] - HEAD_SIZE :] = record
 
 
 def middle(received, chunk, copies, last):
     def kernel(*refs):
-        middle_kernel(last, *refs)
+        middle_kernel(chunk, *refs)
 
     rows, total = received.shape
     width = total - HEAD_SIZE
+    sources = 1 if last else 2
+    shape = (copies * chunk, sources * width + HEAD_SIZE)
     return pl.pallas_call(
         kernel,
         grid=(1,),
-        out_shape=jax.ShapeDtypeStruct((copies * chunk, total), BF16),
+        out_shape=jax.ShapeDtypeStruct(shape, BF16),
         in_specs=[
             pl.BlockSpec((rows, HEAD_SIZE), lambda i: (0, width // HEAD_SIZE)),
-            pl.BlockSpec((chunk, width), lambda i: (0, 0)),
+            pl.BlockSpec((sources * chunk, width), lambda i: (0, 0)),
         ],
-        out_specs=pl.BlockSpec((copies * chunk, total), lambda i: (0, 0)),
+        out_specs=pl.BlockSpec(shape, lambda i: (0, 0)),
         scratch_shapes=[
             pltpu.VMEM((rows, HEAD_SIZE), F32),
             pltpu.VMEM((chunk, HEAD_SIZE), F32),
@@ -293,12 +342,11 @@
                 preferred_element_type=F32,
             )
         out_ref[at:end, head(h)] = (both[:, :HEAD_SIZE] * (1.0 / both[:, HEAD_SIZE:])).astype(BF16)
-        if end == rows:
-            copy = pltpu.make_async_copy(
-                out_ref.at[:, head(h)], out_hbm.at[:, head(h)], sems.at[h]
-            )
-            copy.start()
-            copies.append(copy)
+        copy = pltpu.make_async_copy(
+            out_ref.at[at:end, head(h)], out_hbm.at[at:end, head(h)], sems.at[n]
+        )
+        copy.start()
+        copies.append(copy)
     for copy in copies:
         copy.wait()
 
@@ -317,7 +365,7 @@
         out_specs=pl.BlockSpec(memory_space=pltpu.HBM),
         scratch_shapes=[
             pltpu.VMEM(shape, BF16),
-            pltpu.SemaphoreType.DMA((shape[1] // HEAD_SIZE,)),
+            pltpu.SemaphoreType.DMA((shape[1] // HEAD_SIZE * shape[0] // step,)),
         ],
         compiler_params=pltpu.CompilerParams(vmem_limit_bytes=VMEM_LIMIT),
         name="attend",
@@ -336,8 +384,17 @@
     planes, lines = exchange_groups()
     plane = len(planes[0])
     chunk = rows // 2 // plane
-    inputs = (query_token_query, query_token_key, query_token_value, document_key, document_value)
-    send = local_parts(inputs, rows, width)
+    roots = [planes[0][0], planes[-SIZES[2]][0]]
+    helpers = [planes[0][1], planes[-SIZES[2]][1]]
+    moved = lax.ppermute(document_value, AXES, list(zip(roots, helpers)))
+    inputs = (
+        query_token_query,
+        query_token_key,
+        query_token_value,
+        document_key,
+        document_value,
+    )
+    send = passing_on(local_parts(inputs), moved, helpers)
     received = exchange(send, planes)
     send = middle(received, chunk, len(lines[0]), False)
     received = exchange(send, lines)

time: 74.7 us -> 72.6 us (0.972)
  blocking collectives: 59.1 us -> 51.2 us
  starting transfers between devices: 6.28 us -> 10.2 us
  waiting for transfers between devices: 0.01 us -> 1.85 us
    all_to_all x3, blocking collectives: 59.1 us -> 51.2 us  [exchange(): lax.all_to_all(array, AXES, 0, 0, tiled=True, axis_index_groups=groups)]
    ppermute x0 -> x1, starting transfers between devices: none -> 3.96 us  [body(): moved = lax.ppermute(document_value, AXES, list(zip(roots, helpers)))]
    ppermute x0 -> x1, waiting for transfers between devices: none -> 1.85 us  [body(): moved = lax.ppermute(document_value, AXES, list(zip(roots, helpers)))]
    pallas_call x3 -> x4, Pallas kernels: 1.96 us -> 1.9 us  [the longest x1 1.74 us: local_parts(): pl.pallas_call(local_kernel, out_shape=jax.ShapeDtypeStruct((half, 2 * wi...]
  transfers between devices with their start and end apart: 1 -> 2, of which waited for: 0 -> 1; matrix products, arithmetic and copies ran while one was open for 0% -> 0% of each run, Pallas kernels for 8% -> 10%
where the time goes in v4:
time: 72.6 us; the launch traced here: 72.4 us
  blocking collectives  51.2 us (71%)
  starting transfers between devices  10.2 us (14%)
  Pallas kernels  7.66 us (11%)
  waiting for transfers between devices  1.85 us (3%)
  between operations  0.73 us (1%)
    all_to_all x3, blocking collectives, exchange(): lax.all_to_all(array, AXES, 0, 0, tiled=True, axis_index_groups=groups)  51.2 us
    ppermute x1, starting transfers between devices, body(): other_half = lax.ppermute(answer_half, 'tp', [(0, 1), (1, 0)])  6.27 us
    pallas_call x1, Pallas kernels, attend(): pl.pallas_call(kernel, out_shape=jax.ShapeDtypeStruct(shape, BF16), in_sp...  5.72 us
    ppermute x1, starting transfers between devices, body(): moved = lax.ppermute(document_value, AXES, list(zip(roots, helpers)))  3.96 us
    ppermute x1, waiting for transfers between devices, body(): moved = lax.ppermute(document_value, AXES, list(zip(roots, helpers)))  1.85 us
    pallas_call x1, Pallas kernels, local_parts(): pl.pallas_call(local_kernel, out_shape=jax.ShapeDtypeStruct((half, 2 * wi...  1.74 us
  transfers between devices with their start and end apart: 2, of which 1 were waited for; matrix products, arithmetic and copies ran while one was open for 0% of the time, Pallas kernels for 10%

profile of v4, /device:TPU:1, one launch (start us, length us, event | category | flops | bytes accessed | tf_op | source)
XLA Modules:
  0.0 72.4 jit_solution(3169093868256490634)
XLA Ops:
  0.6 4.0 %collective-permute-start = (bf16[512,256]{1,0:T(8,128)(2,1)}, bf16[512,256]{1,0:T(8,128)(2,1)S(1)}, u32[]{:S(2)}, u32[]{:S(2)}) collective-permute-start(bf16[512,256]{1,0:T(8,128)(2,1)} %refs_3_.1), channel_id=1, source_target_pairs={{0,2},{1,17}} | collective-permute-start | bytes 786440 | tf_op jit(solution)/shard_map/ppermute | solution.py:389
  4.6 1.7 %local_parts.1.send_ref = bf16[256,640]{1,0:T(8,128)(2,1)S(1)} custom-call(bf16[4,1024]{1,0:T(4,128)(2,1)} %qt_hbm.1, bf16[4,256]{1,0:T(4,128)(2,1)} %qk_hbm.1, bf16[4,256]{1,0:T(4,128)(2,1)} %qv_hbm.1, bf16[512,256]{1,0:T(8,128)(2,1)} %refs_2_.1, bf16[512,256]{1,0:T(8,128)(2,1)} %refs_3_.1), custom_call_target="tpu_custom_call" | custom-call | tf_op jit(solution)/shard_map/local_parts/pallas_call | solution.py:164
  6.3 1.9 %collective-permute-done.moved_ref = bf16[512,256]{1,0:T(8,128)(2,1)S(1)} collective-permute-done((bf16[512,256]{1,0:T(8,128)(2,1)}, bf16[512,256]{1,0:T(8,128)(2,1)S(1)}, u32[]{:S(2)}, u32[]{:S(2)}) %collective-permute-start) | collective-permute-done | bytes 262176 | tf_op jit(solution)/shard_map/ppermute | solution.py:389
  8.2 16.1 %all_to_all.33 = bf16[32,8,640]{2,1,0:T(8,128)(2,1)S(1)} all-to-all(bf16[32,8,640]{2,1,0:T(8,128)(2,1)S(1)} %bitcast.10), channel_id=1, replica_groups={{0,2,4,6,8,10,12,14,16,18,20,22,24,26,28,30,32,34,36,38,40,42,44,46,48,..., dimensions={0} | all-to-all | bytes 655360 | tf_op jit(solution)/shard_map/all_to_all | solution.py:40
  24.3 0.1 merge_first.1
  24.4 17.8 %all_to_all.34 = bf16[8,8,1152]{2,1,0:T(8,128)(2,1)S(1)} all-to-all(bf16[8,8,1152]{2,1,0:T(8,128)(2,1)S(1)} %bitcast.14), channel_id=1, replica_groups={{0,64,128,192,256,320,384,448},{2,66,130,194,258,322,386,450},{4,68,132..., dimensions={0} | all-to-all | bytes 294912 | tf_op jit(solution)/shard_map/all_to_all | solution.py:40
  42.1 0.1 merge_last.1
  42.2 0.0 copy-start
  42.2 17.4 %all_to_all.35 = bf16[32,8,1152]{2,1,0:T(8,128)(2,1)S(1)} all-to-all(bf16[32,8,1152]{2,1,0:T(8,128)(2,1)S(1)} %bitcast.11), channel_id=1, replica_groups={{0,2,4,6,8,10,12,14,16,18,20,22,24,26,28,30,32,34,36,38,40,42,44,46,48,..., dimensions={0} | all-to-all | bytes 1179648 | tf_op jit(solution)/shard_map/all_to_all | solution.py:40
  59.6 0.0 copy-start.1
  59.6 0.0 copy-start.2
  59.7 6.3 %collective-permute-start.1 = (bf16[4,1024]{1,0:T(4,128)(2,1)S(1)}, bf16[4,1024]{1,0:T(4,128)(2,1)S(1)}, u32[]{:S(2)}, u32[]{:S(2)}) collective-permute-start(bf16[4,1024]{1,0:T(4,128)(2,1)S(1)} %answer_rows.1), channel_id=1, source_target_pairs={{0,1},{1,0},{2,3},{3,2},{4,5},{5,4},{6,7},{7,6},{8,9},{9,8},{10,11... | collective-permute-start | bytes 24584 | tf_op jit(solution)/shard_map/ppermute | solution.py:404
  65.9 0.0 copy-done
  66.0 0.0 copy-done.1
  66.0 0.0 copy-done.2
  66.0 5.7 %attend.1 = bf16[512,1024]{1,0:T(8,128)(2,1)} custom-call(bf16[512,1024]{1,0:T(8,128)(2,1)S(1)} %copy-done, bf16[256,1152]{1,0:T(8,128)(2,1)S(1)} %bitcast.7, bf16[512,256]{1,0:T(8,128)(2,1)S(1)} %copy-done.1, bf16[512,256]{1,0:T(8,128)(2,1)S(1)} %copy-done.2), custom_call_target="tpu_custom_call" | custom-call | tf_op jit(solution)/shard_map/attend/pallas_call | solution.py:361
  71.7 0.0 collective-permute-done.1
  71.7 0.6 pad_maximum_fusion
  (3 shorter events, 0.0 us)
Async XLA Ops:
  0.6 7.6 %collective-permute-start = (bf16[512,256]{1,0:T(8,128)(2,1)}, bf16[512,256]{1,0:T(8,128)(2,1)S(1)}, u32[]{:S(2)}, u32[]{:S(2)}) collective-permute-start(bf16[512,256]{1,0:T(8,128)(2,1)} %refs_3_.1), channel_id=1, source_target_pairs={{0,2},{1,17}} | collective-permute-start | bytes 786440 | tf_op jit(solution)/shard_map/ppermute | solution.py:389
  42.2 23.7 %copy-start = (bf16[512,1024]{1,0:T(8,128)(2,1)S(1)}, bf16[512,1024]{1,0:T(8,128)(2,1)}, u32[]{:S(2)}) copy-start(bf16[512,1024]{1,0:T(8,128)(2,1)} %refs_0_.1) | copy-start | bytes 3145732
  59.6 6.3 %copy-start.1 = (bf16[512,256]{1,0:T(8,128)(2,1)S(1)}, bf16[512,256]{1,0:T(8,128)(2,1)}, u32[]{:S(2)}) copy-start(bf16[512,256]{1,0:T(8,128)(2,1)} %refs_2_.1) | copy-start | bytes 786436
  59.6 6.3 %copy-start.2 = (bf16[512,256]{1,0:T(8,128)(2,1)S(1)}, bf16[512,256]{1,0:T(8,128)(2,1)}, u32[]{:S(2)}) copy-start(bf16[512,256]{1,0:T(8,128)(2,1)} %refs_3_.1) | copy-start | bytes 786436
  59.7 12.1 %collective-permute-start.1 = (bf16[4,1024]{1,0:T(4,128)(2,1)S(1)}, bf16[4,1024]{1,0:T(4,128)(2,1)S(1)}, u32[]{:S(2)}, u32[]{:S(2)}) collective-permute-start(bf16[4,1024]{1,0:T(4,128)(2,1)S(1)} %answer_rows.1), channel_id=1, source_target_pairs={{0,1},{1,0},{2,3},{3,2},{4,5},{5,4},{6,7},{7,6},{8,9},{9,8},{10,11... | collective-permute-start | bytes 24584 | tf_op jit(solution)/shard_map/ppermute | solution.py:404

commit v5 on v4

--- a/solution.py
+++ b/solution.py
@@ -29,11 +29,11 @@
 def exchange_groups():
     ids = np.arange(2 * math.prod(SIZES)).reshape(SIZES + (2,))
     y, x, z = SIZES
-    first = np.moveaxis(ids[..., 0], 0, -1).reshape(x * z, y)
-    second = ids[..., 1].reshape(y * x, z)
+    first = ids[..., 0].reshape(y * x, z)
+    second = np.moveaxis(ids[..., 1], 0, -1).reshape(x * z, y)
     planes = np.concatenate([first.T, second.T]).tolist()
     lines = np.concatenate([first, second]).tolist()
-    return planes, lines
+    return planes, lines, (planes[0], planes[z])
 
 
 def exchange(array, groups):
@@ -117,7 +117,8 @@
         copy.start()
     rec_ref[...] = jnp.zeros_like(rec_ref)
     first_block = block_index() == 0
-    for copy in copies:
+    qt_copy, k_copy, v_copy, qk_copy, qv_copy = copies
+    for copy in (qt_copy, qk_copy, qv_copy):
         copy.wait()
     heads = qt_ref.shape[1] // HEAD_SIZE
     chunk = half // (heads * QUERY_TOKENS)
@@ -127,29 +128,41 @@
         ].astype(F32)
     group = QUERY_PER_KEY * QUERY_TOKENS
     token = lax.broadcasted_iota(jnp.int32, (group, 1), 0) % QUERY_TOKENS
-    for kv in range(heads // QUERY_PER_KEY):
-        cols = slice(kv * HEAD_SIZE, (kv + 1) * HEAD_SIZE)
-        q = q_ref[kv * group : (kv + 1) * group, :]
-        scores = dot_nt(q.astype(BF16), k_ref[:, cols]) * SCALE
-        new_k = qk_ref[:, cols].astype(F32)
-        new_v = qv_ref[:, cols].astype(F32)
-        own = []
+    groups = range(heads // QUERY_PER_KEY)
+    cols = [slice(kv * HEAD_SIZE, (kv + 1) * HEAD_SIZE) for kv in groups]
+    queries = [q_ref[kv * group : (kv + 1) * group, :] for kv in groups]
+    own = []
+    for kv in groups:
+        new_k = qk_ref[:, cols[kv]].astype(F32)
+        own.append([])
         for j in range(QUERY_TOKENS):
-            s = jnp.sum(q * new_k[j : j + 1, :], axis=-1, keepdims=True) * SCALE
-            own.append(jnp.where(jnp.logical_and(token >= j, first_block), s, NEG))
-        top = jnp.max(scores, axis=-1, keepdims=True)
-        for s in own:
+            s = jnp.sum(queries[kv] * new_k[j : j + 1, :], axis=-1, keepdims=True) * SCALE
+            own[kv].append(jnp.where(jnp.logical_and(token >= j, first_block), s, NEG))
+    k_copy.wait()
+    scores = [dot_nt(queries[kv].astype(BF16), k_ref[:, cols[kv]]) * SCALE for kv in groups]
+    tops = []
+    for kv in groups:
+        top = jnp.max(scores[kv], axis=-1, keepdims=True)
+        for s in own[kv]:
             top = jnp.maximum(top, s)
-        expo = jnp.exp(scores - top)
-        total = jnp.sum(expo, axis=-1, keepdims=True)
-        mixed = jnp.dot(expo.astype(BF16), v_ref[:, cols], preferred_element_type=F32)
-        for j, s in enumerate(own):
-            e = jnp.exp(s - top)
+        tops.append(top)
+    expo = [jnp.exp(scores[kv] - tops[kv]) for kv in groups]
+    v_copy.wait()
+    mixes = [
+        jnp.dot(expo[kv].astype(BF16), v_ref[:, cols[kv]], preferred_element_type=F32)
+        for kv in groups
+    ]
+    full = (group, HEAD_SIZE)
+    for kv in groups:
+        new_v = qv_ref[:, cols[kv]].astype(F32)
+        total = jnp.sum(expo[kv], axis=-1, keepdims=True)
+        mixed = mixes[kv]
+        for j, s in enumerate(own[kv]):
+            e = jnp.exp(s - tops[kv])
             total = total + e
             mixed = mixed + e.astype(BF16).astype(F32) * new_v[j : j + 1, :]
-        full = (group, HEAD_SIZE)
         for k, value in enumerate(
-            record_rows(jnp.broadcast_to(top, full), jnp.broadcast_to(total, full), mixed)
+            record_rows(jnp.broadcast_to(tops[kv], full), jnp.broadcast_to(total, full), mixed)
         ):
             rec_ref[pl.ds(kv * group * chunk + k, group, stride=chunk), :] = value
     out_ref[:, 2 * width :] = rec_ref[...].astype(BF16)
@@ -299,7 +312,7 @@
 STEP = 256
 
 
-def attend_kernel(step, ahead, q_ref, kv_ref, k_ref, v_ref, out_hbm, out_ref, sems):
+def attend_all(step, ahead, q_ref, kv_ref, k_ref, v_ref, out_hbm, out_ref, sems):
     rows = q_ref.shape[0]
     heads = q_ref.shape[1] // HEAD_SIZE
     heads_kv = heads // QUERY_PER_KEY
@@ -351,25 +364,35 @@
         copy.wait()
 
 
-def attend(document_query, received, document_key, document_value, step=STEP, ahead=1):
-    shape = document_query.shape
+def attend(inputs, side, carried, arrived=(), step=STEP, ahead=1):
+    shape = inputs[0].shape
     vmem = pl.BlockSpec(memory_space=pltpu.VMEM)
+    hbm = pl.BlockSpec(memory_space=pltpu.HBM)
+    first = side == 1
 
     def kernel(*refs):
-        attend_kernel(step, ahead, *refs)
-
+        ctx_hbm = refs[5 + len(arrived)]
+        if first:
+            refs[6 + len(arrived)][...] = refs[4][...]
+
+        @pl.when(lax.axis_index("tp") == side)
+        def _():
+            attend_all(step, ahead, *refs[:4], ctx_hbm, *refs[-2:])
+
+    ctx = jax.ShapeDtypeStruct(shape, BF16)
     return pl.pallas_call(
         kernel,
-        out_shape=jax.ShapeDtypeStruct(shape, BF16),
-        in_specs=[vmem] * 4,
-        out_specs=pl.BlockSpec(memory_space=pltpu.HBM),
+        out_shape=(ctx, jax.ShapeDtypeStruct(carried.shape, BF16)) if first else (ctx,),
+        in_specs=[vmem] * 4 + [vmem if first else hbm] + [vmem] * len(arrived),
+        out_specs=(hbm, vmem) if first else (hbm,),
+        input_output_aliases={} if first else {4: 0},
         scratch_shapes=[
             pltpu.VMEM(shape, BF16),
             pltpu.SemaphoreType.DMA((shape[1] // HEAD_SIZE * shape[0] // step,)),
         ],
         compiler_params=pltpu.CompilerParams(vmem_limit_bytes=VMEM_LIMIT),
-        name="attend",
-    )(document_query, received, document_key, document_value)
+        name="attend_tp1" if first else "attend_tp0",
+    )(*inputs, carried, *arrived)
 
 
 def body(
@@ -381,12 +404,11 @@
     query_token_value,
 ):
     rows, width = document_key.shape
-    planes, lines = exchange_groups()
-    plane = len(planes[0])
-    chunk = rows // 2 // plane
-    roots = [planes[0][0], planes[-SIZES[2]][0]]
-    helpers = [planes[0][1], planes[-SIZES[2]][1]]
-    moved = lax.ppermute(document_value, AXES, list(zip(roots, helpers)))
+    planes, lines, root_planes = exchange_groups()
+    peers = len(planes[0])
+    chunk = rows // 2 // peers
+    helpers = [plane[1] for plane in root_planes]
+    moved = lax.ppermute(document_value, AXES, [tuple(plane[:2]) for plane in root_planes])
     inputs = (
         query_token_query,
         query_token_key,
@@ -398,15 +420,18 @@
     received = exchange(send, planes)
     send = middle(received, chunk, len(lines[0]), False)
     received = exchange(send, lines)
-    send = middle(received, chunk, plane, True)
+    send = middle(received, chunk, peers, True)
     received = exchange(send, planes)
     answer_half = answer_rows(received, query_token_query.shape[1])
-    other_half = lax.ppermute(answer_half, "tp", [(0, 1), (1, 0)])
-    ctx_out = attend(document_query, received, document_key, document_value)
+    from_first = lax.ppermute(answer_half, "tp", [(0, 1)])
+    inputs = (document_query, received, document_key, document_value)
+    ctx_out, sent_half = attend(inputs, 1, answer_half)
+    from_second = lax.ppermute(sent_half, "tp", [(1, 0)])
+    (ctx_out,) = attend(inputs, 0, ctx_out, (from_first,))
     first = lax.axis_index("tp") == 0
     halves = (
-        jnp.where(first, answer_half, other_half),
-        jnp.where(first, other_half, answer_half),
+        jnp.where(first, answer_half, from_first),
+        jnp.where(first, from_second, answer_half),
     )
     return (ctx_out, jnp.concatenate(halves, axis=1))
 

time: 72.6 us -> 75.3 us (1.037)
  the two profiles are of different devices: /device:TPU:1 before, /device:TPU:64 now
where the time goes in v5:
time: 75.3 us; the launch traced here: 75 us
  blocking collectives  57.7 us (77%)
  Pallas kernels  7.55 us (10%)
  starting transfers between devices  6.57 us (9%)
  local copies, waits for them, and re-layouts  0.99 us (1%)
  waiting for transfers between devices  0.8 us (1%)
    all_to_all x3, blocking collectives, exchange(): lax.all_to_all(array, AXES, 0, 0, tiled=True, axis_index_groups=groups)  57.7 us
    pallas_call x2, Pallas kernels, attend(): pl.pallas_call(kernel, out_shape=(ctx, jax.ShapeDtypeStruct(carried.shape...  5.85 us
    ppermute x1, starting transfers between devices, body(): from_first = lax.ppermute(answer_half, 'tp', [(0, 1)])  4.6 us
  transfers between devices with their start and end apart: 3, of which 1 were waited for; matrix products, arithmetic and copies ran while one was open for 0% of the time, Pallas kernels for 2%

profile of v5, /device:TPU:64, one launch (start us, length us, event | category | flops | bytes accessed | tf_op | source)
XLA Modules:
  0.0 75.0 jit_solution(15546597738969546153)
XLA Ops:
  0.6 0.7 collective-permute-start
  1.3 1.5 %local_parts.1.send_ref = bf16[256,640]{1,0:T(8,128)(2,1)S(1)} custom-call(bf16[4,1024]{1,0:T(4,128)(2,1)} %qt_hbm.1, bf16[4,256]{1,0:T(4,128)(2,1)} %qk_hbm.1, bf16[4,256]{1,0:T(4,128)(2,1)} %qv_hbm.1, bf16[512,256]{1,0:T(8,128)(2,1)} %refs_2_.3, bf16[512,256]{1,0:T(8,128)(2,1)} %refs_3_.3), custom_call_target="tpu_custom_call" | custom-call | tf_op jit(solution)/shard_map/local_parts/pallas_call | solution.py:177
  2.8 0.0 collective-permute-done.moved_ref
  2.8 21.7 %all_to_all.33 = bf16[32,8,640]{2,1,0:T(8,128)(2,1)S(1)} all-to-all(bf16[32,8,640]{2,1,0:T(8,128)(2,1)S(1)} %bitcast.11), channel_id=1, replica_groups={{0,16,32,48,64,80,96,112,128,144,160,176,192,208,224,240,256,272,288,30..., dimensions={0} | all-to-all | bytes 655360 | tf_op jit(solution)/shard_map/all_to_all | solution.py:40
  24.5 0.1 merge_first.1
  24.6 17.5 %all_to_all.34 = bf16[8,8,1152]{2,1,0:T(8,128)(2,1)S(1)} all-to-all(bf16[8,8,1152]{2,1,0:T(8,128)(2,1)S(1)} %bitcast.15), channel_id=1, replica_groups={{0,2,4,6,8,10,12,14},{16,18,20,22,24,26,28,30},{32,34,36,38,40,42,44,46..., dimensions={0} | all-to-all | bytes 294912 | tf_op jit(solution)/shard_map/all_to_all | solution.py:40
  42.1 0.1 merge_last.1
  42.2 0.0 copy-start
  42.2 18.5 %all_to_all.35 = bf16[32,8,1152]{2,1,0:T(8,128)(2,1)S(1)} all-to-all(bf16[32,8,1152]{2,1,0:T(8,128)(2,1)S(1)} %bitcast.12), channel_id=1, replica_groups={{0,16,32,48,64,80,96,112,128,144,160,176,192,208,224,240,256,272,288,30..., dimensions={0} | all-to-all | bytes 1179648 | tf_op jit(solution)/shard_map/all_to_all | solution.py:40
  60.7 0.0 copy-start.1
  60.7 0.0 copy-start.2
  60.8 0.0 copy-done
  60.8 0.9 %copy-done.1 = bf16[512,256]{1,0:T(8,128)(2,1)S(1)} copy-done((bf16[512,256]{1,0:T(8,128)(2,1)S(1)}, bf16[512,256]{1,0:T(8,128)(2,1)}, u32[]{:S(2)}) %copy-start.1) | copy-done | bytes 262168
  61.7 0.1 copy-done.2
  61.8 0.1 attend_tp1.1
  61.9 1.3 %collective-permute-start.2 = (bf16[4,1024]{1,0:T(4,128)(2,1)S(1)}, bf16[4,1024]{1,0:T(4,128)(2,1)S(1)}, u32[]{:S(2)}, u32[]{:S(2)}) collective-permute-start(bf16[4,1024]{1,0:T(4,128)(2,1)S(1)} %get-tuple-element.5), channel_id=1, source_target_pairs={{1,0},{3,2},{5,4},{7,6},{9,8},{11,10},{13,12},{15,14},{17,16},{19,... | collective-permute-start | bytes 24584 | tf_op jit(solution)/shard_map/ppermute | solution.py:429
  63.2 4.6 %collective-permute-start.1 = (bf16[4,1024]{1,0:T(4,128)(2,1)S(1)}, bf16[4,1024]{1,0:T(4,128)(2,1)S(1)}, u32[]{:S(2)}, u32[]{:S(2)}) collective-permute-start(bf16[4,1024]{1,0:T(4,128)(2,1)S(1)} %answer_rows.1.refs_4_), channel_id=1, source_target_pairs={{0,1},{2,3},{4,5},{6,7},{8,9},{10,11},{12,13},{14,15},{16,17},{18,... | collective-permute-start | bytes 24584 | tf_op jit(solution)/shard_map/ppermute | solution.py:426
  67.8 0.0 collective-permute-done.2
  67.8 0.8 %collective-permute-done.1.refs_5_ = bf16[4,1024]{1,0:T(4,128)(2,1)S(1)} collective-permute-done((bf16[4,1024]{1,0:T(4,128)(2,1)S(1)}, bf16[4,1024]{1,0:T(4,128)(2,1)S(1)}, u32[]{:S(2)}, u32[]{:S(2)}) %collective-permute-start.1) | collective-permute-done | bytes 8224 | tf_op jit(solution)/shard_map/ppermute | solution.py:426
  68.7 0.6 pad_maximum_fusion
  69.3 5.7 %attend_tp0.1 = bf16[512,1024]{1,0:T(8,128)(2,1)} custom-call(bf16[512,1024]{1,0:T(8,128)(2,1)S(1)} %copy-done, bf16[256,1152]{1,0:T(8,128)(2,1)S(1)} %bitcast.8, bf16[512,256]{1,0:T(8,128)(2,1)S(1)} %copy-done.1, bf16[512,256]{1,0:T(8,128)(2,1)S(1)} %copy-done.2, bf16[512,1024]{1,0:T(8,128)(2,1)} %get-tuple-element.4.refs_4_, ...), custom_call_target="tpu_custom_call", output_to_operand_aliasing={{}: (4, {})} | custom-call | tf_op jit(solution)/shard_map/attend_tp0/pallas_call | solution.py:383
  (3 shorter events, 0.1 us)
Async XLA Ops:
  0.6 2.2 %collective-permute-start = (bf16[512,256]{1,0:T(8,128)(2,1)}, bf16[512,256]{1,0:T(8,128)(2,1)S(1)}, u32[]{:S(2)}, u32[]{:S(2)}) collective-permute-start(bf16[512,256]{1,0:T(8,128)(2,1)} %refs_3_.3), channel_id=1, source_target_pairs={{0,16},{1,3}} | collective-permute-start | bytes 786440 | tf_op jit(solution)/shard_map/ppermute | solution.py:411
  42.2 18.6 %copy-start = (bf16[512,1024]{1,0:T(8,128)(2,1)S(1)}, bf16[512,1024]{1,0:T(8,128)(2,1)}, u32[]{:S(2)}) copy-start(bf16[512,1024]{1,0:T(8,128)(2,1)} %refs_0_.3) | copy-start | bytes 3145732
  60.7 1.0 %copy-start.1 = (bf16[512,256]{1,0:T(8,128)(2,1)S(1)}, bf16[512,256]{1,0:T(8,128)(2,1)}, u32[]{:S(2)}) copy-start(bf16[512,256]{1,0:T(8,128)(2,1)} %refs_2_.3) | copy-start | bytes 786436
  60.7 1.0 %copy-start.2 = (bf16[512,256]{1,0:T(8,128)(2,1)S(1)}, bf16[512,256]{1,0:T(8,128)(2,1)}, u32[]{:S(2)}) copy-start(bf16[512,256]{1,0:T(8,128)(2,1)} %refs_3_.3) | copy-start | bytes 786436
  61.9 5.9 %collective-permute-start.2 = (bf16[4,1024]{1,0:T(4,128)(2,1)S(1)}, bf16[4,1024]{1,0:T(4,128)(2,1)S(1)}, u32[]{:S(2)}, u32[]{:S(2)}) collective-permute-start(bf16[4,1024]{1,0:T(4,128)(2,1)S(1)} %get-tuple-element.5), channel_id=1, source_target_pairs={{1,0},{3,2},{5,4},{7,6},{9,8},{11,10},{13,12},{15,14},{17,16},{19,... | collective-permute-start | bytes 24584 | tf_op jit(solution)/shard_map/ppermute | solution.py:429
  63.2 5.4 %collective-permute-start.1 = (bf16[4,1024]{1,0:T(4,128)(2,1)S(1)}, bf16[4,1024]{1,0:T(4,128)(2,1)S(1)}, u32[]{:S(2)}, u32[]{:S(2)}) collective-permute-start(bf16[4,1024]{1,0:T(4,128)(2,1)S(1)} %answer_rows.1.refs_4_), channel_id=1, source_target_pairs={{0,1},{2,3},{4,5},{6,7},{8,9},{10,11},{12,13},{14,15},{16,17},{18,... | collective-permute-start | bytes 24584 | tf_op jit(solution)/shard_map/ppermute | solution.py:426

commit v6 on v5

--- a/solution.py
+++ b/solution.py
@@ -312,7 +312,7 @@
 STEP = 256
 
 
-def attend_all(step, ahead, q_ref, kv_ref, k_ref, v_ref, out_hbm, out_ref, sems):
+def attend_heads(which, step, ahead, q_ref, kv_ref, k_ref, v_ref, out_hbm, out_ref, sems):
     rows = q_ref.shape[0]
     heads = q_ref.shape[1] // HEAD_SIZE
     heads_kv = heads // QUERY_PER_KEY
@@ -323,7 +323,7 @@
     head = lambda n: slice(n * HEAD_SIZE, (n + 1) * HEAD_SIZE)
     far_values = [with_ones(kv_ref[:, head(2 * heads_kv + n)]) for n in range(2 * heads_kv)]
     values = [with_ones(v_ref[:, head(n)]) for n in range(heads_kv)]
-    items = [(h, at) for h in range(heads) for at in range(0, rows, step)]
+    items = [(h, at) for h in which for at in range(0, rows, step)]
     copies = []
 
     def scores_of(h, at):
@@ -364,35 +364,86 @@
         copy.wait()
 
 
-def attend(inputs, side, carried, arrived=(), step=STEP, ahead=1):
-    shape = inputs[0].shape
+def attend_early(document_query, received, document_key, document_value, answer_half):
+    local = (document_query, document_key, document_value)
+    shape = document_query.shape
+    half = shape[1] // HEAD_SIZE // 2
     vmem = pl.BlockSpec(memory_space=pltpu.VMEM)
     hbm = pl.BlockSpec(memory_space=pltpu.HBM)
-    first = side == 1
 
     def kernel(*refs):
-        ctx_hbm = refs[5 + len(arrived)]
-        if first:
-            refs[6 + len(arrived)][...] = refs[4][...]
-
-        @pl.when(lax.axis_index("tp") == side)
+        sources, kv_ref, rows_ref, out_hbm, rows_out_ref = refs[:3], *refs[3:7]
+        targets, out_ref, sems, in_sems = refs[7:10], *refs[10:]
+        rows_out_ref[...] = rows_ref[...]
+
+        @pl.when(lax.axis_index("tp") == 1)
         def _():
-            attend_all(step, ahead, *refs[:4], ctx_hbm, *refs[-2:])
-
-    ctx = jax.ShapeDtypeStruct(shape, BF16)
+            copies = [
+                pltpu.make_async_copy(source, target, in_sems.at[n])
+                for n, (source, target) in enumerate(zip(sources, targets))
+            ]
+            for copy in copies:
+                copy.start()
+            for copy in copies:
+                copy.wait()
+            q_ref, k_ref, v_ref = targets
+            attend_heads(
+                range(half), STEP, 1, q_ref, kv_ref, k_ref, v_ref, out_hbm, out_ref, sems
+            )
+
     return pl.pallas_call(
         kernel,
-        out_shape=(ctx, jax.ShapeDtypeStruct(carried.shape, BF16)) if first else (ctx,),
-        in_specs=[vmem] * 4 + [vmem if first else hbm] + [vmem] * len(arrived),
-        out_specs=(hbm, vmem) if first else (hbm,),
-        input_output_aliases={} if first else {4: 0},
+        out_shape=(
+            jax.ShapeDtypeStruct(shape, BF16),
+            jax.ShapeDtypeStruct(answer_half.shape, BF16),
+        ),
+        in_specs=[hbm] * 3 + [vmem] * 2,
+        out_specs=(hbm, vmem),
+        scratch_shapes=[pltpu.VMEM(array.shape, BF16) for array in local]
+        + [
+            pltpu.VMEM(shape, BF16),
+            pltpu.SemaphoreType.DMA((half * shape[0] // STEP,)),
+            pltpu.SemaphoreType.DMA((3,)),
+        ],
+        compiler_params=pltpu.CompilerParams(vmem_limit_bytes=VMEM_LIMIT),
+        name="attend_early",
+    )(
+        *(pltpu.with_memory_space_constraint(array, pltpu.HBM) for array in local),
+        received,
+        answer_half,
+    )
+
+
+def attend_late(document_query, received, document_key, document_value, ctx_out):
+    shape = document_query.shape
+    heads = shape[1] // HEAD_SIZE
+    vmem = pl.BlockSpec(memory_space=pltpu.VMEM)
+    hbm = pl.BlockSpec(memory_space=pltpu.HBM)
+
+    def kernel(q_ref, kv_ref, k_ref, v_ref, _, out_hbm, out_ref, sems):
+        refs = (q_ref, kv_ref, k_ref, v_ref, out_hbm, out_ref, sems)
+
+        @pl.when(lax.axis_index("tp") == 0)
+        def _():
+            attend_heads(range(heads), STEP, 1, *refs)
+
+        @pl.when(lax.axis_index("tp") == 1)
+        def _():
+            attend_heads(range(heads // 2, heads), STEP, 1, *refs)
+
+    return pl.pallas_call(
+        kernel,
+        out_shape=jax.ShapeDtypeStruct(shape, BF16),
+        in_specs=[vmem] * 4 + [hbm],
+        out_specs=hbm,
+        input_output_aliases={4: 0},
         scratch_shapes=[
             pltpu.VMEM(shape, BF16),
-            pltpu.SemaphoreType.DMA((shape[1] // HEAD_SIZE * shape[0] // step,)),
+            pltpu.SemaphoreType.DMA((heads * shape[0] // STEP,)),
         ],
         compiler_params=pltpu.CompilerParams(vmem_limit_bytes=VMEM_LIMIT),
-        name="attend_tp1" if first else "attend_tp0",
-    )(*inputs, carried, *arrived)
+        name="attend_late",
+    )(document_query, received, document_key, document_value, ctx_out)
 
 
 def body(
@@ -423,15 +474,14 @@
     send = middle(received, chunk, peers, True)
     received = exchange(send, planes)
     answer_half = answer_rows(received, query_token_query.shape[1])
-    from_first = lax.ppermute(answer_half, "tp", [(0, 1)])
     inputs = (document_query, received, document_key, document_value)
-    ctx_out, sent_half = attend(inputs, 1, answer_half)
-    from_second = lax.ppermute(sent_half, "tp", [(1, 0)])
-    (ctx_out,) = attend(inputs, 0, ctx_out, (from_first,))
+    ctx_out, sent_half = attend_early(*inputs, answer_half)
+    other_half = lax.ppermute(sent_half, "tp", [(0, 1), (1, 0)])
+    ctx_out = attend_late(*inputs, ctx_out)
     first = lax.axis_index("tp") == 0
     halves = (
-        jnp.where(first, answer_half, from_first),
-        jnp.where(first, from_second, answer_half),
+        jnp.where(first, answer_half, other_half),
+        jnp.where(first, other_half, answer_half),
     )
     return (ctx_out, jnp.concatenate(halves, axis=1))
 

time: 75.3 us -> 71.3 us (0.947)
  the two profiles are of different devices: /device:TPU:64 before, /device:TPU:1 now
where the time goes in v6:
time: 71.3 us; the launch traced here: 70.5 us
  blocking collectives  49.4 us (69%)
  Pallas kernels  10.2 us (14%)
  starting transfers between devices  7.4 us (10%)
  waiting for transfers between devices  2.11 us (3%)
  between operations  0.75 us (1%)
    all_to_all x3, blocking collectives, exchange(): lax.all_to_all(array, AXES, 0, 0, tiled=True, axis_index_groups=groups)  49.4 us
    pallas_call x1, Pallas kernels, attend_early(): pl.pallas_call(kernel, out_shape=(jax.ShapeDtypeStruct(shape, BF16), jax....  4.85 us
    ppermute x1, starting transfers between devices, body(): lax.ppermute(document_value, AXES, [tuple(plane[:2]) for plane in root_pl...  4.84 us
    pallas_call x1, Pallas kernels, attend_late(): pl.pallas_call(kernel, out_shape=jax.ShapeDtypeStruct(shape, BF16), in_sp...  3.64 us
    ppermute x1, starting transfers between devices, body(): other_half = lax.ppermute(sent_half, 'tp', [(0, 1), (1, 0)])  2.56 us
    ppermute x1, waiting for transfers between devices, body(): lax.ppermute(document_value, AXES, [tuple(plane[:2]) for plane in root_pl...  2.11 us
    pallas_call x1, Pallas kernels, local_parts(): pl.pallas_call(local_kernel, out_shape=jax.ShapeDtypeStruct((half, 2 * wi...  1.48 us
  transfers between devices with their start and end apart: 2, of which 1 were waited for; matrix products, arithmetic and copies ran while one was open for 0% of the time, Pallas kernels for 7%

profile of v6, /device:TPU:1, one launch (start us, length us, event | category | flops | bytes accessed | tf_op | source)
XLA Modules:
  0.0 70.5 jit_solution(14585761196362734133)
XLA Ops:
  0.6 4.8 %collective-permute-start = (bf16[512,256]{1,0:T(8,128)(2,1)}, bf16[512,256]{1,0:T(8,128)(2,1)S(1)}, u32[]{:S(2)}, u32[]{:S(2)}) collective-permute-start(bf16[512,256]{1,0:T(8,128)(2,1)} %v_ref.1), channel_id=1, source_target_pairs={{0,16},{1,3}} | collective-permute-start | bytes 786440 | tf_op jit(solution)/shard_map/ppermute | solution.py:462
  5.5 1.5 %local_parts.1.send_ref = bf16[256,640]{1,0:T(8,128)(2,1)S(1)} custom-call(bf16[4,1024]{1,0:T(4,128)(2,1)} %qt_hbm.1, bf16[4,256]{1,0:T(4,128)(2,1)} %qk_hbm.1, bf16[4,256]{1,0:T(4,128)(2,1)} %qv_hbm.1, bf16[512,256]{1,0:T(8,128)(2,1)} %k_ref.1, bf16[512,256]{1,0:T(8,128)(2,1)} %v_ref.1), custom_call_target="tpu_custom_call" | custom-call | tf_op jit(solution)/shard_map/local_parts/pallas_call | solution.py:177
  7.0 2.1 %collective-permute-done.moved_ref = bf16[512,256]{1,0:T(8,128)(2,1)S(1)} collective-permute-done((bf16[512,256]{1,0:T(8,128)(2,1)}, bf16[512,256]{1,0:T(8,128)(2,1)S(1)}, u32[]{:S(2)}, u32[]{:S(2)}) %collective-permute-start) | collective-permute-done | bytes 262176 | tf_op jit(solution)/shard_map/ppermute | solution.py:462
  9.1 17.2 %all_to_all.33 = bf16[32,8,640]{2,1,0:T(8,128)(2,1)S(1)} all-to-all(bf16[32,8,640]{2,1,0:T(8,128)(2,1)S(1)} %bitcast.11), channel_id=1, replica_groups={{0,16,32,48,64,80,96,112,128,144,160,176,192,208,224,240,256,272,288,30..., dimensions={0} | all-to-all | bytes 655360 | tf_op jit(solution)/shard_map/all_to_all | solution.py:40
  26.3 0.1 merge_first.1
  26.4 14.7 %all_to_all.34 = bf16[8,8,1152]{2,1,0:T(8,128)(2,1)S(1)} all-to-all(bf16[8,8,1152]{2,1,0:T(8,128)(2,1)S(1)} %bitcast.15), channel_id=1, replica_groups={{0,2,4,6,8,10,12,14},{16,18,20,22,24,26,28,30},{32,34,36,38,40,42,44,46..., dimensions={0} | all-to-all | bytes 294912 | tf_op jit(solution)/shard_map/all_to_all | solution.py:40
  41.1 0.1 merge_last.1
  41.2 17.5 %all_to_all.35 = bf16[32,8,1152]{2,1,0:T(8,128)(2,1)S(1)} all-to-all(bf16[32,8,1152]{2,1,0:T(8,128)(2,1)S(1)} %bitcast.12), channel_id=1, replica_groups={{0,16,32,48,64,80,96,112,128,144,160,176,192,208,224,240,256,272,288,30..., dimensions={0} | all-to-all | bytes 1179648 | tf_op jit(solution)/shard_map/all_to_all | solution.py:40
  58.7 0.0 copy-start
  58.7 0.0 copy-start.1
  58.7 0.0 copy-start.2
  58.7 4.9 %attend_early.1 = (bf16[512,1024]{1,0:T(8,128)(2,1)}, bf16[4,1024]{1,0:T(4,128)(2,1)S(1)}) custom-call(bf16[512,1024]{1,0:T(8,128)(2,1)} %q_ref.1, bf16[512,256]{1,0:T(8,128)(2,1)} %k_ref.1, bf16[512,256]{1,0:T(8,128)(2,1)} %v_ref.1, bf16[256,1152]{1,0:T(8,128)(2,1)S(1)} %bitcast.7, bf16[4,1024]{1,0:T(4,128)(2,1)S(1)} %answer_rows.1.refs_4_), custom_call_target="tpu_custom_call" | custom-call | tf_op jit(solution)/shard_map/attend_early/pallas_call | solution.py:394
  63.6 2.6 %collective-permute-start.1 = (bf16[4,1024]{1,0:T(4,128)(2,1)S(1)}, bf16[4,1024]{1,0:T(4,128)(2,1)S(1)}, u32[]{:S(2)}, u32[]{:S(2)}) collective-permute-start(bf16[4,1024]{1,0:T(4,128)(2,1)S(1)} %get-tuple-element.5), channel_id=1, source_target_pairs={{0,1},{1,0},{2,3},{3,2},{4,5},{5,4},{6,7},{7,6},{8,9},{9,8},{10,11... | collective-permute-start | bytes 24584 | tf_op jit(solution)/shard_map/ppermute | solution.py:479
  66.1 0.0 copy-done
  66.2 0.0 copy-done.1
  66.2 0.0 copy-done.2
  66.2 3.6 %attend_late.1 = bf16[512,1024]{1,0:T(8,128)(2,1)} custom-call(bf16[512,1024]{1,0:T(8,128)(2,1)S(1)} %copy-done, bf16[256,1152]{1,0:T(8,128)(2,1)S(1)} %bitcast.8, bf16[512,256]{1,0:T(8,128)(2,1)S(1)} %copy-done.1, bf16[512,256]{1,0:T(8,128)(2,1)S(1)} %copy-done.2, bf16[512,1024]{1,0:T(8,128)(2,1)} %get-tuple-element.4._), custom_call_target="tpu_custom_call", output_to_operand_aliasing={{}: (4, {})} | custom-call | tf_op jit(solution)/shard_map/attend_late/pallas_call | solution.py:434
  69.8 0.0 collective-permute-done.1
  69.9 0.6 pad_maximum_fusion
  (3 shorter events, 0.0 us)
Async XLA Ops:
  0.6 8.5 %collective-permute-start = (bf16[512,256]{1,0:T(8,128)(2,1)}, bf16[512,256]{1,0:T(8,128)(2,1)S(1)}, u32[]{:S(2)}, u32[]{:S(2)}) collective-permute-start(bf16[512,256]{1,0:T(8,128)(2,1)} %v_ref.1), channel_id=1, source_target_pairs={{0,16},{1,3}} | collective-permute-start | bytes 786440 | tf_op jit(solution)/shard_map/ppermute | solution.py:462
  58.7 7.5 %copy-start = (bf16[512,1024]{1,0:T(8,128)(2,1)S(1)}, bf16[512,1024]{1,0:T(8,128)(2,1)}, u32[]{:S(2)}) copy-start(bf16[512,1024]{1,0:T(8,128)(2,1)} %q_ref.1) | copy-start | bytes 3145732
  58.7 7.5 %copy-start.1 = (bf16[512,256]{1,0:T(8,128)(2,1)S(1)}, bf16[512,256]{1,0:T(8,128)(2,1)}, u32[]{:S(2)}) copy-start(bf16[512,256]{1,0:T(8,128)(2,1)} %k_ref.1) | copy-start | bytes 786436
  58.7 7.5 %copy-start.2 = (bf16[512,256]{1,0:T(8,128)(2,1)S(1)}, bf16[512,256]{1,0:T(8,128)(2,1)}, u32[]{:S(2)}) copy-start(bf16[512,256]{1,0:T(8,128)(2,1)} %v_ref.1) | copy-start | bytes 786436
  63.6 6.3 %collective-permute-start.1 = (bf16[4,1024]{1,0:T(4,128)(2,1)S(1)}, bf16[4,1024]{1,0:T(4,128)(2,1)S(1)}, u32[]{:S(2)}, u32[]{:S(2)}) collective-permute-start(bf16[4,1024]{1,0:T(4,128)(2,1)S(1)} %get-tuple-element.5), channel_id=1, source_target_pairs={{0,1},{1,0},{2,3},{3,2},{4,5},{5,4},{6,7},{7,6},{8,9},{9,8},{10,11... | collective-permute-start | bytes 24584 | tf_op jit(solution)/shard_map/ppermute | solution.py:479

commit v7 on v6

--- a/solution.py
+++ b/solution.py
@@ -379,7 +379,11 @@
         @pl.when(lax.axis_index("tp") == 1)
         def _():
             copies = [
-                pltpu.make_async_copy(source, target, in_sems.at[n])
+                pltpu.make_async_copy(
+                    source.at[:, : source.shape[1] // 2],
+                    target.at[:, : source.shape[1] // 2],
+                    in_sems.at[n],
+                )
                 for n, (source, target) in enumerate(zip(sources, targets))
             ]
             for copy in copies:

time: 71.3 us -> 71.1 us (level)
  no operation moved by 1% of the time
where the time goes in v7:
time: 71.1 us; the launch traced here: 70.5 us
  blocking collectives  49.4 us (69%)
  Pallas kernels  9.94 us (14%)
  starting transfers between devices  7.65 us (11%)
  waiting for transfers between devices  2.11 us (3%)
  between operations  0.75 us (1%)
    all_to_all x3, blocking collectives, exchange(): lax.all_to_all(array, AXES, 0, 0, tiled=True, axis_index_groups=groups)  49.4 us
    ppermute x1, starting transfers between devices, body(): lax.ppermute(document_value, AXES, [tuple(plane[:2]) for plane in root_pl...  4.84 us
    pallas_call x1, Pallas kernels, attend_early(): pl.pallas_call(kernel, out_shape=(jax.ShapeDtypeStruct(shape, BF16), jax....  4.61 us
    pallas_call x1, Pallas kernels, attend_late(): pl.pallas_call(kernel, out_shape=jax.ShapeDtypeStruct(shape, BF16), in_sp...  3.64 us
    ppermute x1, starting transfers between devices, body(): other_half = lax.ppermute(sent_half, 'tp', [(0, 1), (1, 0)])  2.8 us
    ppermute x1, waiting for transfers between devices, body(): lax.ppermute(document_value, AXES, [tuple(plane[:2]) for plane in root_pl...  2.11 us
    pallas_call x1, Pallas kernels, local_parts(): pl.pallas_call(local_kernel, out_shape=jax.ShapeDtypeStruct((half, 2 * wi...  1.48 us
  transfers between devices with their start and end apart: 2, of which 1 were waited for; matrix products, arithmetic and copies ran while one was open for 0% of the time, Pallas kernels for 7%

profile of v7, /device:TPU:1, one launch (start us, length us, event | category | flops | bytes accessed | tf_op | source)
XLA Modules:
  0.0 70.5 jit_solution(9066188015020765583)
XLA Ops:
  0.6 4.8 %collective-permute-start = (bf16[512,256]{1,0:T(8,128)(2,1)}, bf16[512,256]{1,0:T(8,128)(2,1)S(1)}, u32[]{:S(2)}, u32[]{:S(2)}) collective-permute-start(bf16[512,256]{1,0:T(8,128)(2,1)} %v_ref.1), channel_id=1, source_target_pairs={{0,16},{1,3}} | collective-permute-start | bytes 786440 | tf_op jit(solution)/shard_map/ppermute | solution.py:466
  5.5 1.5 %local_parts.1.send_ref = bf16[256,640]{1,0:T(8,128)(2,1)S(1)} custom-call(bf16[4,1024]{1,0:T(4,128)(2,1)} %qt_hbm.1, bf16[4,256]{1,0:T(4,128)(2,1)} %qk_hbm.1, bf16[4,256]{1,0:T(4,128)(2,1)} %qv_hbm.1, bf16[512,256]{1,0:T(8,128)(2,1)} %k_ref.1, bf16[512,256]{1,0:T(8,128)(2,1)} %v_ref.1), custom_call_target="tpu_custom_call" | custom-call | tf_op jit(solution)/shard_map/local_parts/pallas_call | solution.py:177
  7.0 2.1 %collective-permute-done.moved_ref = bf16[512,256]{1,0:T(8,128)(2,1)S(1)} collective-permute-done((bf16[512,256]{1,0:T(8,128)(2,1)}, bf16[512,256]{1,0:T(8,128)(2,1)S(1)}, u32[]{:S(2)}, u32[]{:S(2)}) %collective-permute-start) | collective-permute-done | bytes 262176 | tf_op jit(solution)/shard_map/ppermute | solution.py:466
  9.1 17.2 %all_to_all.33 = bf16[32,8,640]{2,1,0:T(8,128)(2,1)S(1)} all-to-all(bf16[32,8,640]{2,1,0:T(8,128)(2,1)S(1)} %bitcast.11), channel_id=1, replica_groups={{0,16,32,48,64,80,96,112,128,144,160,176,192,208,224,240,256,272,288,30..., dimensions={0} | all-to-all | bytes 655360 | tf_op jit(solution)/shard_map/all_to_all | solution.py:40
  26.3 0.1 merge_first.1
  26.4 14.7 %all_to_all.34 = bf16[8,8,1152]{2,1,0:T(8,128)(2,1)S(1)} all-to-all(bf16[8,8,1152]{2,1,0:T(8,128)(2,1)S(1)} %bitcast.15), channel_id=1, replica_groups={{0,2,4,6,8,10,12,14},{16,18,20,22,24,26,28,30},{32,34,36,38,40,42,44,46..., dimensions={0} | all-to-all | bytes 294912 | tf_op jit(solution)/shard_map/all_to_all | solution.py:40
  41.1 0.1 merge_last.1
  41.2 17.5 %all_to_all.35 = bf16[32,8,1152]{2,1,0:T(8,128)(2,1)S(1)} all-to-all(bf16[32,8,1152]{2,1,0:T(8,128)(2,1)S(1)} %bitcast.12), channel_id=1, replica_groups={{0,16,32,48,64,80,96,112,128,144,160,176,192,208,224,240,256,272,288,30..., dimensions={0} | all-to-all | bytes 1179648 | tf_op jit(solution)/shard_map/all_to_all | solution.py:40
  58.7 0.0 copy-start
  58.7 0.0 copy-start.1
  58.7 0.0 copy-start.2
  58.7 4.6 %attend_early.1 = (bf16[512,1024]{1,0:T(8,128)(2,1)}, bf16[4,1024]{1,0:T(4,128)(2,1)S(1)}) custom-call(bf16[512,1024]{1,0:T(8,128)(2,1)} %q_ref.1, bf16[512,256]{1,0:T(8,128)(2,1)} %k_ref.1, bf16[512,256]{1,0:T(8,128)(2,1)} %v_ref.1, bf16[256,1152]{1,0:T(8,128)(2,1)S(1)} %bitcast.7, bf16[4,1024]{1,0:T(4,128)(2,1)S(1)} %answer_rows.1.refs_4_), custom_call_target="tpu_custom_call" | custom-call | tf_op jit(solution)/shard_map/attend_early/pallas_call | solution.py:398
  63.3 2.8 %collective-permute-start.1 = (bf16[4,1024]{1,0:T(4,128)(2,1)S(1)}, bf16[4,1024]{1,0:T(4,128)(2,1)S(1)}, u32[]{:S(2)}, u32[]{:S(2)}) collective-permute-start(bf16[4,1024]{1,0:T(4,128)(2,1)S(1)} %get-tuple-element.5), channel_id=1, source_target_pairs={{0,1},{1,0},{2,3},{3,2},{4,5},{5,4},{6,7},{7,6},{8,9},{9,8},{10,11... | collective-permute-start | bytes 24584 | tf_op jit(solution)/shard_map/ppermute | solution.py:483
  66.1 0.0 copy-done
  66.2 0.0 copy-done.1
  66.2 0.0 copy-done.2
  66.2 3.6 %attend_late.1 = bf16[512,1024]{1,0:T(8,128)(2,1)} custom-call(bf16[512,1024]{1,0:T(8,128)(2,1)S(1)} %copy-done, bf16[256,1152]{1,0:T(8,128)(2,1)S(1)} %bitcast.8, bf16[512,256]{1,0:T(8,128)(2,1)S(1)} %copy-done.1, bf16[512,256]{1,0:T(8,128)(2,1)S(1)} %copy-done.2, bf16[512,1024]{1,0:T(8,128)(2,1)} %get-tuple-element.4._), custom_call_target="tpu_custom_call", output_to_operand_aliasing={{}: (4, {})} | custom-call | tf_op jit(solution)/shard_map/attend_late/pallas_call | solution.py:438
  69.8 0.0 collective-permute-done.1
  69.9 0.6 pad_maximum_fusion
  (3 shorter events, 0.0 us)
Async XLA Ops:
  0.6 8.5 %collective-permute-start = (bf16[512,256]{1,0:T(8,128)(2,1)}, bf16[512,256]{1,0:T(8,128)(2,1)S(1)}, u32[]{:S(2)}, u32[]{:S(2)}) collective-permute-start(bf16[512,256]{1,0:T(8,128)(2,1)} %v_ref.1), channel_id=1, source_target_pairs={{0,16},{1,3}} | collective-permute-start | bytes 786440 | tf_op jit(solution)/shard_map/ppermute | solution.py:466
  58.7 7.5 %copy-start = (bf16[512,1024]{1,0:T(8,128)(2,1)S(1)}, bf16[512,1024]{1,0:T(8,128)(2,1)}, u32[]{:S(2)}) copy-start(bf16[512,1024]{1,0:T(8,128)(2,1)} %q_ref.1) | copy-start | bytes 3145732
  58.7 7.5 %copy-start.1 = (bf16[512,256]{1,0:T(8,128)(2,1)S(1)}, bf16[512,256]{1,0:T(8,128)(2,1)}, u32[]{:S(2)}) copy-start(bf16[512,256]{1,0:T(8,128)(2,1)} %k_ref.1) | copy-start | bytes 786436
  58.7 7.5 %copy-start.2 = (bf16[512,256]{1,0:T(8,128)(2,1)S(1)}, bf16[512,256]{1,0:T(8,128)(2,1)}, u32[]{:S(2)}) copy-start(bf16[512,256]{1,0:T(8,128)(2,1)} %v_ref.1) | copy-start | bytes 786436
  63.3 6.5 %collective-permute-start.1 = (bf16[4,1024]{1,0:T(4,128)(2,1)S(1)}, bf16[4,1024]{1,0:T(4,128)(2,1)S(1)}, u32[]{:S(2)}, u32[]{:S(2)}) collective-permute-start(bf16[4,1024]{1,0:T(4,128)(2,1)S(1)} %get-tuple-element.5), channel_id=1, source_target_pairs={{0,1},{1,0},{2,3},{3,2},{4,5},{5,4},{6,7},{7,6},{8,9},{9,8},{10,11... | collective-permute-start | bytes 24584 | tf_op jit(solution)/shard_map/ppermute | solution.py:483

commit v8 on v6

--- a/solution.py
+++ b/solution.py
@@ -312,7 +312,9 @@
 STEP = 256
 
 
-def attend_heads(which, step, ahead, q_ref, kv_ref, k_ref, v_ref, out_hbm, out_ref, sems):
+def attend_heads(
+    which, step, ahead, q_ref, kv_ref, k_ref, v_ref, out_hbm, out_ref, sems, loads=()
+):
     rows = q_ref.shape[0]
     heads = q_ref.shape[1] // HEAD_SIZE
     heads_kv = heads // QUERY_PER_KEY
@@ -328,6 +330,8 @@
 
     def scores_of(h, at):
         kv = h // QUERY_PER_KEY
+        if loads and at == 0:
+            loads[h].wait()
         q = q_ref[at : at + step, head(h)]
         return (
             dot_nt(q, kv_ref[:, head(kv)]),
@@ -371,25 +375,31 @@
     vmem = pl.BlockSpec(memory_space=pltpu.VMEM)
     hbm = pl.BlockSpec(memory_space=pltpu.HBM)
 
-    def kernel(*refs):
-        sources, kv_ref, rows_ref, out_hbm, rows_out_ref = refs[:3], *refs[3:7]
-        targets, out_ref, sems, in_sems = refs[7:10], *refs[10:]
+    def kernel(*args):
+        sources, kv_ref, rows_ref, out_hbm, rows_out_ref = args[:3], *args[3:7]
+        targets, out_ref, sems, in_sems = args[7:10], *args[10:]
         rows_out_ref[...] = rows_ref[...]
 
         @pl.when(lax.axis_index("tp") == 1)
         def _():
+            q_ref, k_ref, v_ref = targets
+            pairs = [
+                (source.at[:, : source.shape[1] // 2], target.at[:, : source.shape[1] // 2])
+                for source, target in zip(sources[1:], targets[1:])
+            ]
+            for h in range(half):
+                cols = slice(h * HEAD_SIZE, (h + 1) * HEAD_SIZE)
+                pairs.append((sources[0].at[:, cols], q_ref.at[:, cols]))
             copies = [
                 pltpu.make_async_copy(source, target, in_sems.at[n])
-                for n, (source, target) in enumerate(zip(sources, targets))
+                for n, (source, target) in enumerate(pairs)
             ]
             for copy in copies:
                 copy.start()
-            for copy in copies:
+            for copy in copies[:2]:
                 copy.wait()
-            q_ref, k_ref, v_ref = targets
-            attend_heads(
-                range(half), STEP, 1, q_ref, kv_ref, k_ref, v_ref, out_hbm, out_ref, sems
-            )
+            refs = (q_ref, kv_ref, k_ref, v_ref, out_hbm, out_ref, sems)
+            attend_heads(range(half), STEP, 1, *refs, loads=copies[2:])
 
     return pl.pallas_call(
         kernel,
@@ -403,7 +413,7 @@
         + [
             pltpu.VMEM(shape, BF16),
             pltpu.SemaphoreType.DMA((half * shape[0] // STEP,)),
-            pltpu.SemaphoreType.DMA((3,)),
+            pltpu.SemaphoreType.DMA((2 + half,)),
         ],
         compiler_params=pltpu.CompilerParams(vmem_limit_bytes=VMEM_LIMIT),
         name="attend_early",

time: 71.3 us -> 71.8 us (level)
  no operation moved by 1% of the time
where the time goes in v8:
time: 71.8 us; the launch traced here: 70.5 us
  blocking collectives  49.4 us (69%)
  Pallas kernels  10.7 us (15%)
  starting transfers between devices  6.89 us (10%)
  waiting for transfers between devices  2.11 us (3%)
  between operations  0.75 us (1%)
    all_to_all x3, blocking collectives, exchange(): lax.all_to_all(array, AXES, 0, 0, tiled=True, axis_index_groups=groups)  49.4 us
    pallas_call x1, Pallas kernels, attend_early(): pl.pallas_call(kernel, out_shape=(jax.ShapeDtypeStruct(shape, BF16), jax....  5.39 us
    ppermute x1, starting transfers between devices, body(): lax.ppermute(document_value, AXES, [tuple(plane[:2]) for plane in root_pl...  4.84 us
    pallas_call x1, Pallas kernels, attend_late(): pl.pallas_call(kernel, out_shape=jax.ShapeDtypeStruct(shape, BF16), in_sp...  3.64 us
    ppermute x1, waiting for transfers between devices, body(): lax.ppermute(document_value, AXES, [tuple(plane[:2]) for plane in root_pl...  2.11 us
    ppermute x1, starting transfers between devices, body(): other_half = lax.ppermute(sent_half, 'tp', [(0, 1), (1, 0)])  2.05 us
    pallas_call x1, Pallas kernels, local_parts(): pl.pallas_call(local_kernel, out_shape=jax.ShapeDtypeStruct((half, 2 * wi...  1.48 us
  transfers between devices with their start and end apart: 2, of which 1 were waited for; matrix products, arithmetic and copies ran while one was open for 0% of the time, Pallas kernels for 7%

profile of v8, /device:TPU:1, one launch (start us, length us, event | category | flops | bytes accessed | tf_op | source)
XLA Modules:
  0.0 70.5 jit_solution(9682178378949520074)
XLA Ops:
  0.6 4.8 %collective-permute-start = (bf16[512,256]{1,0:T(8,128)(2,1)}, bf16[512,256]{1,0:T(8,128)(2,1)S(1)}, u32[]{:S(2)}, u32[]{:S(2)}) collective-permute-start(bf16[512,256]{1,0:T(8,128)(2,1)} %v_ref.1), channel_id=1, source_target_pairs={{0,16},{1,3}} | collective-permute-start | bytes 786440 | tf_op jit(solution)/shard_map/ppermute | solution.py:472
  5.5 1.5 %local_parts.1.send_ref = bf16[256,640]{1,0:T(8,128)(2,1)S(1)} custom-call(bf16[4,1024]{1,0:T(4,128)(2,1)} %qt_hbm.1, bf16[4,256]{1,0:T(4,128)(2,1)} %qk_hbm.1, bf16[4,256]{1,0:T(4,128)(2,1)} %qv_hbm.1, bf16[512,256]{1,0:T(8,128)(2,1)} %k_ref.1, bf16[512,256]{1,0:T(8,128)(2,1)} %v_ref.1), custom_call_target="tpu_custom_call" | custom-call | tf_op jit(solution)/shard_map/local_parts/pallas_call | solution.py:177
  7.0 2.1 %collective-permute-done.moved_ref = bf16[512,256]{1,0:T(8,128)(2,1)S(1)} collective-permute-done((bf16[512,256]{1,0:T(8,128)(2,1)}, bf16[512,256]{1,0:T(8,128)(2,1)S(1)}, u32[]{:S(2)}, u32[]{:S(2)}) %collective-permute-start) | collective-permute-done | bytes 262176 | tf_op jit(solution)/shard_map/ppermute | solution.py:472
  9.1 17.2 %all_to_all.33 = bf16[32,8,640]{2,1,0:T(8,128)(2,1)S(1)} all-to-all(bf16[32,8,640]{2,1,0:T(8,128)(2,1)S(1)} %bitcast.11), channel_id=1, replica_groups={{0,16,32,48,64,80,96,112,128,144,160,176,192,208,224,240,256,272,288,30..., dimensions={0} | all-to-all | bytes 655360 | tf_op jit(solution)/shard_map/all_to_all | solution.py:40
  26.3 0.1 merge_first.1
  26.4 14.7 %all_to_all.34 = bf16[8,8,1152]{2,1,0:T(8,128)(2,1)S(1)} all-to-all(bf16[8,8,1152]{2,1,0:T(8,128)(2,1)S(1)} %bitcast.15), channel_id=1, replica_groups={{0,2,4,6,8,10,12,14},{16,18,20,22,24,26,28,30},{32,34,36,38,40,42,44,46..., dimensions={0} | all-to-all | bytes 294912 | tf_op jit(solution)/shard_map/all_to_all | solution.py:40
  41.1 0.1 merge_last.1
  41.2 17.5 %all_to_all.35 = bf16[32,8,1152]{2,1,0:T(8,128)(2,1)S(1)} all-to-all(bf16[32,8,1152]{2,1,0:T(8,128)(2,1)S(1)} %bitcast.12), channel_id=1, replica_groups={{0,16,32,48,64,80,96,112,128,144,160,176,192,208,224,240,256,272,288,30..., dimensions={0} | all-to-all | bytes 1179648 | tf_op jit(solution)/shard_map/all_to_all | solution.py:40
  58.7 0.0 copy-start
  58.7 0.0 copy-start.1
  58.7 0.0 copy-start.2
  58.7 5.4 %attend_early.1 = (bf16[512,1024]{1,0:T(8,128)(2,1)}, bf16[4,1024]{1,0:T(4,128)(2,1)S(1)}) custom-call(bf16[512,1024]{1,0:T(8,128)(2,1)} %q_ref.1, bf16[512,256]{1,0:T(8,128)(2,1)} %k_ref.1, bf16[512,256]{1,0:T(8,128)(2,1)} %v_ref.1, bf16[256,1152]{1,0:T(8,128)(2,1)S(1)} %bitcast.7, bf16[4,1024]{1,0:T(4,128)(2,1)S(1)} %answer_rows.1.args_4_), custom_call_target="tpu_custom_call" | custom-call | tf_op jit(solution)/shard_map/attend_early/pallas_call | solution.py:404
  64.1 2.0 %collective-permute-start.1 = (bf16[4,1024]{1,0:T(4,128)(2,1)S(1)}, bf16[4,1024]{1,0:T(4,128)(2,1)S(1)}, u32[]{:S(2)}, u32[]{:S(2)}) collective-permute-start(bf16[4,1024]{1,0:T(4,128)(2,1)S(1)} %get-tuple-element.5), channel_id=1, source_target_pairs={{0,1},{1,0},{2,3},{3,2},{4,5},{5,4},{6,7},{7,6},{8,9},{9,8},{10,11... | collective-permute-start | bytes 24584 | tf_op jit(solution)/shard_map/ppermute | solution.py:489
  66.2 0.0 copy-done
  66.2 0.0 copy-done.1
  66.2 0.0 copy-done.2
  66.2 3.6 %attend_late.1 = bf16[512,1024]{1,0:T(8,128)(2,1)} custom-call(bf16[512,1024]{1,0:T(8,128)(2,1)S(1)} %copy-done, bf16[256,1152]{1,0:T(8,128)(2,1)S(1)} %bitcast.8, bf16[512,256]{1,0:T(8,128)(2,1)S(1)} %copy-done.1, bf16[512,256]{1,0:T(8,128)(2,1)S(1)} %copy-done.2, bf16[512,1024]{1,0:T(8,128)(2,1)} %get-tuple-element.4._), custom_call_target="tpu_custom_call", output_to_operand_aliasing={{}: (4, {})} | custom-call | tf_op jit(solution)/shard_map/attend_late/pallas_call | solution.py:444
  69.9 0.0 collective-permute-done.1
  69.9 0.6 pad_maximum_fusion
  (3 shorter events, 0.0 us)
Async XLA Ops:
  0.6 8.5 %collective-permute-start = (bf16[512,256]{1,0:T(8,128)(2,1)}, bf16[512,256]{1,0:T(8,128)(2,1)S(1)}, u32[]{:S(2)}, u32[]{:S(2)}) collective-permute-start(bf16[512,256]{1,0:T(8,128)(2,1)} %v_ref.1), channel_id=1, source_target_pairs={{0,16},{1,3}} | collective-permute-start | bytes 786440 | tf_op jit(solution)/shard_map/ppermute | solution.py:472
  58.7 7.5 %copy-start = (bf16[512,1024]{1,0:T(8,128)(2,1)S(1)}, bf16[512,1024]{1,0:T(8,128)(2,1)}, u32[]{:S(2)}) copy-start(bf16[512,1024]{1,0:T(8,128)(2,1)} %q_ref.1) | copy-start | bytes 3145732
  58.7 7.5 %copy-start.1 = (bf16[512,256]{1,0:T(8,128)(2,1)S(1)}, bf16[512,256]{1,0:T(8,128)(2,1)}, u32[]{:S(2)}) copy-start(bf16[512,256]{1,0:T(8,128)(2,1)} %k_ref.1) | copy-start | bytes 786436
  58.7 7.5 %copy-start.2 = (bf16[512,256]{1,0:T(8,128)(2,1)S(1)}, bf16[512,256]{1,0:T(8,128)(2,1)}, u32[]{:S(2)}) copy-start(bf16[512,256]{1,0:T(8,128)(2,1)} %v_ref.1) | copy-start | bytes 786436
  64.1 5.7 %collective-permute-start.1 = (bf16[4,1024]{1,0:T(4,128)(2,1)S(1)}, bf16[4,1024]{1,0:T(4,128)(2,1)S(1)}, u32[]{:S(2)}, u32[]{:S(2)}) collective-permute-start(bf16[4,1024]{1,0:T(4,128)(2,1)S(1)} %get-tuple-element.5), channel_id=1, source_target_pairs={{0,1},{1,0},{2,3},{3,2},{4,5},{5,4},{6,7},{7,6},{8,9},{9,8},{10,11... | collective-permute-start | bytes 24584 | tf_op jit(solution)/shard_map/ppermute | solution.py:489
